TPU v7x, 32 devices: a whole 2x2x4 slice. The times are simulated.
32 devices in a mesh: shard: 2 (over core), heads: 4 (over y, x), tensor: 4 (over z).
Axes of the slice: x: 2, y: 2, z: 4, core: 2. Of those that a mesh axis runs over, the one named last changes fastest.
Arguments:
- tokens: bfloat16 [8, 2048, 768], P(('shard', 'tensor'), 'heads'), may hold values from -6 to 6
- ln1_gain: bfloat16 [768], P('shard'), may hold values from 0.5 to 1.5
- ln1_bias: bfloat16 [768], P('shard'), may hold values from -2 to 2
- w_qkv: bfloat16 [768, 2304], P('shard'), may hold values from -0.21875 to 0.21875
- bias_qv: bfloat16 [2, 768], P(None, 'shard'), may hold values from -2 to 2
- w_out: bfloat16 [768, 768], P('shard'), may hold values from -0.875 to 0.875
- bias_out: bfloat16 [768], P('shard'), may hold values from -2 to 2
- ln2_gain: bfloat16 [768], P('shard'), may hold values from 0.5 to 1.5
- ln2_bias: bfloat16 [768], P('shard'), may hold values from -2 to 2
- w_in: bfloat16 [3072, 768], P(('shard', 'tensor')), may hold values from -0.21875 to 0.21875
- bias_in: bfloat16 [3072], P(('shard', 'tensor')), may hold values from -2 to 2
- w_back: bfloat16 [3072, 768], P(('shard', 'tensor')), may hold values from -0.109375 to 0.109375
- bias_back: bfloat16 [768], P('shard'), may hold values from -2 to 2
- seq_lengths: int32 [8, 4], P(('shard', 'tensor')), may hold values from 1 to 1024, 2048 in all within a row
- cotangent: bfloat16 [8, 2048, 768], P(('shard', 'tensor'), 'heads'), may hold values from -6 to 6
Outputs:
- output: bfloat16 [8, 2048, 768], P(('shard', 'tensor'), 'heads')
- input_grad: bfloat16 [8, 2048, 768], P(('shard', 'tensor'), 'heads')
- grad_ln1_gain: float32 [768], P('shard')
- grad_ln1_bias: float32 [768], P('shard')
- grad_w_qkv: float32 [768, 2304], P('shard')
- grad_bias_qv: float32 [2, 768], P(None, 'shard')
- grad_w_out: float32 [768, 768], P('shard')
- grad_bias_out: float32 [768], P('shard')
- grad_ln2_gain: float32 [768], P('shard')
- grad_ln2_bias: float32 [768], P('shard')
- grad_w_in: float32 [3072, 768], P(('shard', 'tensor'))
- grad_bias_in: float32 [3072], P(('shard', 'tensor'))
- grad_w_back: float32 [3072, 768], P(('shard', 'tensor'))
- grad_bias_back: float32 [768], P('shard')
Inputs may be any that keep to these rules, and one draw needn't show every extreme that they name: `seq_lengths`: each row sums to 2048, and its largest length is exactly 1024.
All inputs are finite; a program needn't handle non-finite values.
Results may differ from a plain program's by a relative error of at most 0.012.
Values may be sent and summed in bfloat16 or wider, within the bound.
A program may use at most 128 MiB of HBM per device.

v0:
```python
import math

import jax
import jax.numpy as jnp
from jax import lax
from jax.sharding import PartitionSpec as P

HEAD_DIM = 64


EPSILON = 1e-05
NEGATIVE = -1e30


def layer_norm(values, gain, shift):
    center = jnp.mean(values, axis=-1, keepdims=True)
    offset = values - center
    spread = jnp.mean(offset * offset, axis=-1, keepdims=True)
    return offset * lax.rsqrt(spread + EPSILON) * gain + shift


def gelu_tanh(values):
    return jax.nn.gelu(values, approximate=True)


def contract_last(left, right):
    return lax.dot_general(
        left, right, (((1,), (1,)), ((), ())), preferred_element_type=jnp.float32
    )


def contract_first(left, right):
    return lax.dot_general(
        left, right, (((0,), (0,)), ((), ())), preferred_element_type=jnp.float32
    )


def segment_ids(lengths, count):
    ends = jnp.cumsum(lengths)
    positions = jnp.arange(count, dtype=jnp.int32)
    return jnp.sum((ends[None, :] <= positions[:, None]).astype(jnp.int32), axis=1)


def masked_scores(query_block, keys, segment, start, scale):
    block = query_block.shape[0]
    group_len = keys.shape[0]
    scores = contract_last(query_block, keys) * scale
    query_pos = start + jnp.arange(block, dtype=jnp.int32)
    key_pos = jnp.arange(group_len, dtype=jnp.int32)
    seg_block = lax.dynamic_slice_in_dim(segment, start, block, 0)
    allowed = (seg_block[:, None] == segment[None, :]) & (key_pos[None, :] <= query_pos[:, None])
    return jnp.where(allowed, scores, NEGATIVE)


def attend(queries, keys, values, segment, block, scale):
    group_len = keys.shape[0]

    def one_block(number):
        start = number * block
        query_block = lax.dynamic_slice_in_dim(queries, start, block, 0)
        scores = masked_scores(query_block, keys, segment, start, scale)
        largest = jnp.max(scores, axis=1, keepdims=True)
        weights = jnp.exp(scores - largest)
        totals = jnp.sum(weights, axis=1, keepdims=True)
        probs = (weights / totals).astype(jnp.bfloat16)
        attended = jnp.dot(probs, values, preferred_element_type=jnp.float32)
        return (attended, largest[:, 0] + jnp.log(totals[:, 0]))

    attended, log_total = lax.map(one_block, jnp.arange(group_len // block, dtype=jnp.int32))
    return (attended.reshape(group_len, -1), log_total.reshape(group_len))


def attend_back(queries, keys, values, grad_out, log_total, segment, block, scale):
    group_len, head_width = keys.shape

    def one_block(carry, number):
        grad_keys, grad_values = carry
        start = number * block
        query_block = lax.dynamic_slice_in_dim(queries, start, block, 0)
        grad_block = lax.dynamic_slice_in_dim(grad_out, start, block, 0)
        total_block = lax.dynamic_slice_in_dim(log_total, start, block, 0)
        scores = masked_scores(query_block, keys, segment, start, scale)
        probs = jnp.exp(scores - total_block[:, None])
        grad_probs = contract_last(grad_block, values)
        weighted = jnp.sum(probs * grad_probs, axis=1, keepdims=True)
        grad_scores = (probs * (grad_probs - weighted)).astype(jnp.bfloat16)
        grad_query = jnp.dot(grad_scores, keys, preferred_element_type=jnp.float32) * scale
        grad_keys = grad_keys + contract_first(grad_scores, query_block) * scale
        grad_values = grad_values + contract_first(probs.astype(jnp.bfloat16), grad_block)
        return ((grad_keys, grad_values), grad_query)

    empty = jnp.zeros((group_len, head_width), jnp.float32)
    totals, grad_query = lax.scan(
        one_block, (empty, empty), jnp.arange(group_len // block, dtype=jnp.int32)
    )
    return (grad_query.reshape(group_len, head_width), totals[0], totals[1])


def local(
    tokens,
    ln1_gain,
    ln1_bias,
    w_qkv,
    bias_qv,
    w_out,
    bias_out,
    ln2_gain,
    ln2_bias,
    w_in,
    bias_in,
    w_back,
    bias_back,
    seq_lengths,
    cotangent,
):
    gathered = (
        lax.all_gather(ln1_gain, "shard", axis=0, tiled=True),
        lax.all_gather(ln1_bias, "shard", axis=0, tiled=True),
        lax.all_gather(w_qkv, "shard", axis=0, tiled=True),
        lax.all_gather(bias_qv, "shard", axis=1, tiled=True),
        lax.all_gather(w_out, "shard", axis=0, tiled=True),
        lax.all_gather(bias_out, "shard", axis=0, tiled=True),
        lax.all_gather(ln2_gain, "shard", axis=0, tiled=True),
        lax.all_gather(ln2_bias, "shard", axis=0, tiled=True),
        lax.all_gather(w_in, "shard", axis=0, tiled=True),
        lax.all_gather(bias_in, "shard", axis=0, tiled=True),
        lax.all_gather(w_back, "shard", axis=0, tiled=True),
        lax.all_gather(bias_back, "shard", axis=0, tiled=True),
    )
    (
        gain_one,
        shift_one,
        full_qkv,
        qv_bias,
        full_out,
        out_bias,
        gain_two,
        shift_two,
        full_in,
        in_bias,
        full_back,
        back_bias,
    ) = gathered
    tok_count = tokens.shape[1]
    width = tokens.shape[2]
    inputs = tokens[0].astype(jnp.float32)
    normed_one, norm_one_back = jax.vjp(
        layer_norm, inputs, gain_one.astype(jnp.float32), shift_one.astype(jnp.float32)
    )
    attn_in = normed_one.astype(jnp.bfloat16)
    qkv_bias = jnp.concatenate(
        [
            qv_bias[0].astype(jnp.float32),
            jnp.zeros((width,), jnp.float32),
            qv_bias[1].astype(jnp.float32),
        ]
    )
    projected = (jnp.dot(attn_in, full_qkv, preferred_element_type=jnp.float32) + qkv_bias).astype(
        jnp.bfloat16
    )
    heads_in = lax.all_to_all(
        projected.reshape(tok_count, 3, width), "heads", split_axis=2, concat_axis=0, tiled=True
    )
    group_len = heads_in.shape[0]
    local_width = heads_in.shape[2]
    segment = segment_ids(seq_lengths[0], group_len)
    head_count = local_width // HEAD_DIM
    block = min(512, group_len)
    scale = 1.0 / math.sqrt(HEAD_DIM)
    attended_list = []
    total_list = []
    for head_num in range(head_count):
        first = head_num * HEAD_DIM
        attended_head, total_head = attend(
            heads_in[:, 0, first : first + HEAD_DIM],
            heads_in[:, 1, first : first + HEAD_DIM],
            heads_in[:, 2, first : first + HEAD_DIM],
            segment,
            block,
            scale,
        )
        attended_list.append(attended_head)
        total_list.append(total_head)
    attended = jnp.concatenate(attended_list, axis=1).astype(jnp.bfloat16)
    back_tok = lax.all_to_all(attended, "heads", split_axis=0, concat_axis=1, tiled=True)
    hidden_res = (
        inputs
        + jnp.dot(back_tok, full_out, preferred_element_type=jnp.float32)
        + out_bias.astype(jnp.float32)
    )
    normed_two, norm_two_back = jax.vjp(
        layer_norm, hidden_res, gain_two.astype(jnp.float32), shift_two.astype(jnp.float32)
    )
    mlp_in = normed_two.astype(jnp.bfloat16)
    cot_rows = cotangent[0]
    mlp_rows, cot_all = (
        lax.all_gather(mlp_in, "tensor", axis=0, tiled=True),
        lax.all_gather(cot_rows, "tensor", axis=0, tiled=True),
    )
    pre_act = contract_last(mlp_rows, full_in) + in_bias.astype(jnp.float32)
    activated, gelu_back = jax.vjp(gelu_tanh, pre_act)
    act_low = activated.astype(jnp.bfloat16)
    partial_out = jnp.dot(act_low, full_back, preferred_element_type=jnp.float32)
    branch = lax.psum_scatter(
        partial_out.astype(jnp.bfloat16), "tensor", scatter_dimension=0, tiled=True
    ).astype(jnp.float32)
    result = hidden_res + branch + back_bias.astype(jnp.float32)
    output = result.astype(jnp.bfloat16)[None]
    cot_float = cot_rows.astype(jnp.float32)
    grad_back_bias = jnp.sum(cot_float, axis=0)
    grad_w_back = contract_first(act_low, cot_all)
    grad_act = contract_last(cot_all, full_back)
    grad_pre = gelu_back(grad_act)[0].astype(jnp.bfloat16)
    grad_in_bias = jnp.sum(grad_pre.astype(jnp.float32), axis=0)
    grad_w_in = contract_first(grad_pre, mlp_rows)
    grad_mlp_part = jnp.dot(grad_pre, full_in, preferred_element_type=jnp.float32)
    grad_normed_two = lax.psum_scatter(grad_mlp_part, "tensor", scatter_dimension=0, tiled=True)
    grad_res_norm, grad_gain_two, grad_shift_two = norm_two_back(grad_normed_two)
    grad_hidden = cot_float + grad_res_norm
    hidden_low = grad_hidden.astype(jnp.bfloat16)
    grad_out_bias = jnp.sum(hidden_low.astype(jnp.float32), axis=0)
    grad_w_out = contract_first(back_tok, hidden_low)
    grad_attended = contract_last(hidden_low, full_out).astype(jnp.bfloat16)
    grad_heads = lax.all_to_all(grad_attended, "heads", split_axis=1, concat_axis=0, tiled=True)
    query_grads = []
    key_grads = []
    value_grads = []
    for head_num in range(head_count):
        first = head_num * HEAD_DIM
        grad_query, grad_keys, grad_values = attend_back(
            heads_in[:, 0, first : first + HEAD_DIM],
            heads_in[:, 1, first : first + HEAD_DIM],
            heads_in[:, 2, first : first + HEAD_DIM],
            grad_heads[:, first : first + HEAD_DIM],
            total_list[head_num],
            segment,
            block,
            scale,
        )
        query_grads.append(grad_query)
        key_grads.append(grad_keys)
        value_grads.append(grad_values)
    stacked = jnp.stack(
        [
            jnp.concatenate(query_grads, axis=1),
            jnp.concatenate(key_grads, axis=1),
            jnp.concatenate(value_grads, axis=1),
        ],
        axis=1,
    ).astype(jnp.bfloat16)
    grad_proj = lax.all_to_all(stacked, "heads", split_axis=0, concat_axis=2, tiled=True).reshape(
        tok_count, 3 * width
    )
    grad_w_qkv = contract_first(attn_in, grad_proj)
    grad_proj_float = grad_proj.astype(jnp.float32)
    grad_qv_bias = jnp.stack(
        [
            jnp.sum(grad_proj_float[:, :width], axis=0),
            jnp.sum(grad_proj_float[:, 2 * width :], axis=0),
        ]
    )
    grad_attn_in = contract_last(grad_proj, full_qkv)
    grad_input_norm, grad_gain_one, grad_shift_one = norm_one_back(grad_attn_in)
    input_grad = (grad_hidden + grad_input_norm).astype(jnp.bfloat16)[None]
    summed_attn = lax.psum(
        (
            grad_gain_one,
            grad_shift_one,
            grad_w_qkv,
            grad_qv_bias,
            grad_w_out,
            grad_out_bias,
            grad_gain_two,
            grad_shift_two,
            grad_back_bias,
        ),
        ("heads", "tensor"),
    )
    summed_mlp = lax.psum((grad_w_in, grad_in_bias, grad_w_back), "heads")
    owned = (
        lax.psum_scatter(summed_attn[0], "shard", scatter_dimension=0, tiled=True),
        lax.psum_scatter(summed_attn[1], "shard", scatter_dimension=0, tiled=True),
        lax.psum_scatter(summed_attn[2], "shard", scatter_dimension=0, tiled=True),
        lax.psum_scatter(summed_attn[3], "shard", scatter_dimension=1, tiled=True),
        lax.psum_scatter(summed_attn[4], "shard", scatter_dimension=0, tiled=True),
        lax.psum_scatter(summed_attn[5], "shard", scatter_dimension=0, tiled=True),
        lax.psum_scatter(summed_attn[6], "shard", scatter_dimension=0, tiled=True),
        lax.psum_scatter(summed_attn[7], "shard", scatter_dimension=0, tiled=True),
        lax.psum_scatter(summed_attn[8], "shard", scatter_dimension=0, tiled=True),
        lax.psum_scatter(summed_mlp[0], "shard", scatter_dimension=0, tiled=True),
        lax.psum_scatter(summed_mlp[1], "shard", scatter_dimension=0, tiled=True),
        lax.psum_scatter(summed_mlp[2], "shard", scatter_dimension=0, tiled=True),
    )
    return (
        output,
        input_grad,
        owned[0],
        owned[1],
        owned[2],
        owned[3],
        owned[4],
        owned[5],
        owned[6],
        owned[7],
        owned[9],
        owned[10],
        owned[11],
        owned[8],
    )


def solution(mesh):
    in_specs = (
        P(("shard", "tensor"), "heads", None),
        P("shard"),
        P("shard"),
        P("shard", None),
        P(None, "shard"),
        P("shard", None),
        P("shard"),
        P("shard"),
        P("shard"),
        P(("shard", "tensor"), None),
        P(("shard", "tensor")),
        P(("shard", "tensor"), None),
        P("shard"),
        P(("shard", "tensor"), None),
        P(("shard", "tensor"), "heads", None),
    )
    out_specs = (
        P(("shard", "tensor"), "heads", None),
        P(("shard", "tensor"), "heads", None),
        P("shard"),
        P("shard"),
        P("shard", None),
        P(None, "shard"),
        P("shard", None),
        P("shard"),
        P("shard"),
        P("shard"),
        P(("shard", "tensor"), None),
        P(("shard", "tensor")),
        P(("shard", "tensor"), None),
        P("shard"),
    )
    return jax.shard_map(local, mesh=mesh, in_specs=in_specs, out_specs=out_specs, check_vma=False)
```

profile of v0, /device:TPU:0, one launch (start us, length us, event | category | flops | bytes accessed | tf_op | source)
XLA Modules:
  0.0 1142.8 jit_solution(2648171563191227272)
XLA Ops:
  16.8 8.2 all-gather.15.cloned.1.call-done
  25.0 5.6 fusion.70
  30.6 4.3 copy.132
  34.9 5.4 copy.133
  40.3 4.8 all-to-all-start
  46.1 35.9 %all-to-all-done = bf16[512,3,768]{0,1,2:T(4,128)(2,1)} async-done(((bf16[512,3,768]{0,1,2:T(4,128)(2,1)}), bf16[512,3,768]{0,1,2:T(4,128)(2,1)}, u32[]{:S(2)}, u32[]{:S(2)}) %all-to-all-start) | async-done | bytes 2359328 | tf_op jit(solution)/shard_map/all_to_all | solution.py:161
  86.8 34.0 %while.81 = (s32[]{:T(128)}, bf16[4,512,64]{1,2,0:T(8,128)(2,1)S(1)}, f32[4,512]{1,0:T(4,128)S(1)}, s32[4]{0:T(128)S(1)}, s32[2048]{0:T(1024)S(1)}, /*index=5*/b...) while((s32[]{:T(128)}, ...), condition=%wide.region_7.8_spmd, body=%wide.region_4.7_spmd.sunk | while | flops 279969792 | bytes 30709984 | solution.py:69
  92.1 3.2 fusion.222
  100.6 3.2 fusion.222
  109.1 3.2 fusion.222
  117.6 3.2 fusion.222
  126.1 36.4 %while.82 = (s32[]{:T(128)}, bf16[4,512,64]{1,2,0:T(8,128)(2,1)}, f32[4,512]{1,0:T(4,128)S(1)}, s32[4]{0:T(128)S(1)}, s32[2048]{0:T(1024)S(1)}, /*index=5*/bf16[...) while((s32[]{:T(128)}, bf16[4,512,64]{1,2,0:T(8,128)(2,1)}, ...), condition=%wide.region_11.12_spmd, body=%wide.region_8.11_spmd.sunk | while | flops 279969792 | bytes 30448348 | solution.py:69
  131.4 3.8 fusion.227
  140.5 3.8 fusion.227
  149.5 3.8 fusion.227
  158.6 3.8 fusion.227
  166.0 36.4 %while.83 = (s32[]{:T(128)}, bf16[4,512,64]{1,2,0:T(8,128)(2,1)}, f32[4,512]{1,0:T(4,128)S(1)}, s32[4]{0:T(128)S(1)}, s32[2048]{0:T(1024)S(1)}, /*index=5*/bf16[...) while((s32[]{:T(128)}, bf16[4,512,64]{1,2,0:T(8,128)(2,1)}, ...), condition=%wide.region_15.16_spmd, body=%wide.region_12.15_spmd.sunk | while | flops 279969792 | bytes 30448348 | solution.py:69
  171.3 3.8 fusion.232
  180.4 3.8 fusion.232
  189.5 3.8 fusion.232
  198.6 3.8 fusion.232
  204.6 4.2 all-to-all-start.1
  215.5 4.1 all-to-all-done.1
  226.8 61.9 %all-gather.19.cloned.1.call-done = bf16[2048,768]{1,0:T(8,128)(2,1)} async-done(((bf16[512,768]{1,0:T(8,128)(2,1)}), bf16[2048,768]{1,0:T(8,128)(2,1)}) %all-gather.19.cloned.1.call-update) | async-done | bytes 3145744 | tf_op jit(solution)/shard_map/all_gather | solution.py:197
  288.8 7.5 fusion.124
  298.1 66.1 %all-gather.25.cloned.1.call-done = bf16[1,2048,768]{2,1,0:T(8,128)(2,1)} async-done(((bf16[1,512,768]{2,1,0:T(8,128)(2,1)}), bf16[1,2048,768]{2,1,0:T(8,128)(2,1)}) %all-gather.25.cloned.1.call-update) | async-done | bytes 3145744 | tf_op jit(solution)/shard_map/all_gather | solution.py:198
  364.2 9.8 convert_reduce_fusion
  375.7 5.7 fusion.125
  381.7 8.8 convolution_convert_fusion
  390.6 7.0 fusion.127
  397.7 8.7 fusion.71
  408.2 82.8 %reduce-scatter.12.cloned.1.call-done = f32[512,768]{1,0:T(8,128)} async-done(((f32[2048,768]{1,0:T(8,128)}), f32[512,768]{1,0:T(8,128)}) %reduce-scatter.12.cloned.1.call-update) | async-done | bytes 1572880 | tf_op jit(solution)/shard_map/reduce_scatter | solution.py:217
  493.6 61.1 %reduce-scatter.10.cloned.1.call-done = bf16[512,768]{1,0:T(8,128)(2,1)} async-done(((bf16[2048,768]{1,0:T(8,128)(2,1)}), bf16[512,768]{1,0:T(8,128)(2,1)}) %reduce-scatter.10.cloned.1.call-update) | async-done | bytes 786448 | tf_op jit(solution)/shard_map/reduce_scatter | solution.py:204
  554.7 3.2 fusion.118
  562.0 3.6 all-to-all-start.2
  565.7 3.4 fusion.126
  569.3 7.0 all-to-all-done.2
  578.0 59.7 %while.84 = (s32[]{:T(128)}, f32[2048,64]{0,1:T(8,128)}, f32[2048,64]{0,1:T(8,128)}, bf16[4,512,64]{1,2,0:T(8,128)(2,1)}, s32[4]{0:T(128)S(1)}, /*index=5*/s32[2...) while((s32[]{:T(128)}, f32[2048,64]{0,1:T(8,128)}, ...), condition=%wide.region_24.25_spmd.clone, body=%wide.region_22.24_spmd.clone.sunk | while | flops 684359680 | bytes 72119168 | solution.py:93
  580.1 3.0 multiply_reduce_fusion.9
  594.7 3.0 multiply_reduce_fusion.9
  609.8 3.0 multiply_reduce_fusion.9
  624.8 3.0 multiply_reduce_fusion.9
  638.4 62.6 %while.85 = (s32[]{:T(128)}, f32[2048,64]{0,1:T(8,128)}, f32[2048,64]{0,1:T(8,128)}, bf16[4,512,64]{1,2,0:T(8,128)(2,1)}, s32[4]{0:T(128)S(1)}, /*index=5*/s32[2...) while((s32[]{:T(128)}, f32[2048,64]{0,1:T(8,128)}, ...), condition=%wide.region_27.28_spmd.clone, body=%wide.region_25.27_spmd.clone.sunk | while | flops 684359680 | bytes 69759808 | solution.py:93
  641.4 3.0 multiply_reduce_fusion.10
  656.7 3.0 multiply_reduce_fusion.10
  672.5 3.0 multiply_reduce_fusion.10
  688.2 3.0 multiply_reduce_fusion.10
  701.7 55.5 %while.86 = (s32[]{:T(128)}, f32[2048,64]{0,1:T(8,128)}, f32[2048,64]{0,1:T(8,128)}, bf16[4,512,64]{1,2,0:T(8,128)(2,1)}, s32[4]{0:T(128)S(1)}, /*index=5*/s32[2...) while((s32[]{:T(128)}, f32[2048,64]{0,1:T(8,128)}, ...), condition=%wide.region_30.31_spmd.clone, body=%wide.region_28.30_spmd.clone.sunk | while | flops 684359680 | bytes 74216312 | solution.py:93
  703.9 3.0 multiply_reduce_fusion.11
  717.6 3.0 multiply_reduce_fusion.11
  731.5 3.0 multiply_reduce_fusion.11
  745.5 3.0 multiply_reduce_fusion.11
  765.2 4.7 copy.162
  769.9 53.2 %all_to_all.68 = bf16[2048,3,192]{2,1,0:T(4,128)(2,1)} all-to-all(bf16[2048,3,192]{2,1,0:T(4,128)(2,1)} %copy.162), channel_id=1, replica_groups=mesh['shard'=2,'heads'=4,'tensor'=4] {'heads'}, dimensions={0} | all-to-all | bytes 4718592 | tf_op jit(solution)/shard_map/all_to_all | solution.py:251
  823.2 7.0 copy.164
  830.2 6.9 fusion.100
  841.4 10.3 reduce-scatter.14.cloned.1.call-done
  853.2 5.0 fusion.116
  860.1 3.4 all-reduce.10
  864.1 10.7 psum.105
  874.9 3.2 fusion.98
  879.1 76.5 %all-reduce.7 = (f32[384]{0:T(512)}, f32[384]{0:T(512)}, f32[2,384]{1,0:T(2,128)}, f32[384]{0:T(512)}, f32[384]{0:T(512)}, /*index=5*/f32[384]{0:T(512)}, f32[384]{0:T(512)}) all-reduce(f32[384]{0:T(512)S(1)} %dynamic-slice.1, f32[384]{0:T(512)S(1)} %dynamic-slice.3, ...), channel_id=1, replica_groups=mesh['shard'=2,'heads'=4,'tensor'=4] {'heads','tensor'}, use_global_device_ids=true, to_apply=%region_34.35 | all-reduce | flops 3072 | bytes 24576 | tf_op jit(solution)/shard_map/psum | solution.py:265
  955.7 172.9 %all-reduce.14.cloned.1.call-done = (f32[384,2304]{1,0:T(8,128)}, f32[384,768]{1,0:T(8,128)}) async-done(((f32[384,2304]{1,0:T(8,128)}, f32[384,768]{1,0:T(8,128)}), (f32[384,2304]{1,0:T(8,128)}, f32[384,768]{1,0:T(8,128)})) %all-reduce.14.cloned.1.call-update) | async-done | bytes 4718608 | tf_op jit(solution)/shard_map/psum | solution.py:265
  1128.6 4.2 copy.256
  (582 shorter events, 263.9 us)
Async XLA Ops:
  7.2 9.2 copy-start.26
  7.2 17.8 %all-gather.15.cloned.1.call-start = ((), (), s32[]{:S(2)}) async-start(), calls=%async_computation.11 | async-start | bytes 5308416 | tf_op jit(solution)/shard_map/all_gather | solution.py:119
  10.6 20.0 %copy-start.42 = (f32[768]{0:T(1024)}, f32[768]{0:T(1024)S(1)}, u32[]{:S(2)}) copy-start(f32[768]{0:T(1024)S(1)} %reshape.329) | copy-start | bytes 9220
  13.1 17.5 %copy-start.56 = (f32[768]{0:T(1024)}, f32[768]{0:T(1024)S(1)}, u32[]{:S(2)}) copy-start(f32[768]{0:T(1024)S(1)} %reshape.330) | copy-start | bytes 9220
  16.4 14.2 %copy-start.44 = (f32[512]{0:T(512)}, f32[512]{0:T(512)S(1)}, u32[]{:S(2)}) copy-start(f32[512]{0:T(512)S(1)} %broadcast_multiply_fusion.1) | copy-start | bytes 6148
  16.7 13.9 %copy-start.48 = (f32[512]{0:T(512)}, f32[512]{0:T(512)S(1)}, u32[]{:S(2)}) copy-start(f32[512]{0:T(512)S(1)} %fusion.89) | copy-start | bytes 6148
  16.8 13.8 %copy-start.46 = (f32[512]{0:T(512)}, f32[512]{0:T(512)S(1)}, u32[]{:S(2)}) copy-start(f32[512]{0:T(512)S(1)} %fusion.113) | copy-start | bytes 6148
  40.3 5.5 copy-start.64
  40.3 41.7 %all-to-all-start = ((bf16[512,3,768]{0,1,2:T(4,128)(2,1)}), bf16[512,3,768]{0,1,2:T(4,128)(2,1)}, u32[]{:S(2)}, u32[]{:S(2)}) async-start(bf16[512,3,768]{0,1,2:T(4,128)(2,1)} %copy.133), calls=%async_computation | async-start | bytes 6291456 | tf_op jit(solution)/shard_map/all_to_all | solution.py:161
  45.0 170.4 %all-gather.17.cloned.1.call-start = ((), (), s32[]{:S(2)}) async-start(), calls=%async_computation.12 | async-start | bytes 1769472 | tf_op jit(solution)/shard_map/all_gather | solution.py:121
  166.0 36.4 %copy-start.40 = (bf16[4,512,64]{1,2,0:T(8,128)(2,1)S(1)}, bf16[4,512,64]{1,2,0:T(8,128)(2,1)}, u32[]{:S(2)}) copy-start(bf16[4,512,64]{1,2,0:T(8,128)(2,1)} %copy-done.39) | copy-start | bytes 786436
  166.0 36.4 %copy-start.41 = (bf16[4,512,64]{1,2,0:T(8,128)(2,1)S(1)}, bf16[4,512,64]{1,2,0:T(8,128)(2,1)}, u32[]{:S(2)}) copy-start(bf16[4,512,64]{1,2,0:T(8,128)(2,1)} %get-tuple-element.321) | copy-start | bytes 786436
  202.4 17.3 %copy-start.9 = (bf16[2048,64]{1,0:T(8,128)(2,1)}, bf16[2048,64]{1,0:T(8,128)(2,1)S(1)}, u32[]{:S(2)}) copy-start(bf16[2048,64]{1,0:T(8,128)(2,1)S(1)} %get-tuple-element.1500) | copy-start | bytes 786436
  202.4 17.3 %copy-start.16 = (bf16[2048,64]{1,0:T(8,128)(2,1)}, bf16[2048,64]{1,0:T(8,128)(2,1)S(1)}, u32[]{:S(2)}) copy-start(bf16[2048,64]{1,0:T(8,128)(2,1)S(1)} %get-tuple-element.1503) | copy-start | bytes 786436
  202.4 17.3 %copy-start.33 = (bf16[2048,64]{1,0:T(8,128)(2,1)}, bf16[2048,64]{1,0:T(8,128)(2,1)S(1)}, u32[]{:S(2)}) copy-start(bf16[2048,64]{1,0:T(8,128)(2,1)S(1)} %get-tuple-element.1545) | copy-start | bytes 786436
  202.4 7.2 copy-start.58
  202.4 9.0 copy-start.59
  202.4 10.8 copy-start.60
  204.6 15.0 %all-to-all-start.1 = ((bf16[4,512,192]{1,2,0:T(8,128)(2,1)}), bf16[4,512,192]{1,2,0:T(8,128)(2,1)}, u32[]{:S(2)}, u32[]{:S(2)}) async-start(bf16[4,512,192]{1,2,0:T(8,128)(2,1)} %pad_maximum_fusion.1), calls=%async_computation.1 | async-start | bytes 1572864 | tf_op jit(solution)/shard_map/all_to_all | solution.py:185
  208.8 18.1 %all-gather.21.cloned.1.call-start = ((), (), s32[]{:S(2)}) async-start(), calls=%async_computation.14 | async-start | bytes 1769472 | tf_op jit(solution)/shard_map/all_gather | solution.py:125
  209.5 79.3 %all-gather.19.cloned.1.call-start = ((), (), s32[]{:S(2)}) async-start(), calls=%async_computation.13 | async-start | bytes 3932160 | tf_op jit(solution)/shard_map/all_gather | solution.py:197
  223.8 74.3 %all-gather.23.cloned.1.call-start = ((), (), s32[]{:S(2)}) async-start(), calls=%async_computation.15 | async-start | bytes 1769472 | tf_op jit(solution)/shard_map/all_gather | solution.py:127
  224.3 139.8 %all-gather.25.cloned.1.call-start = ((), (), s32[]{:S(2)}) async-start(), calls=%async_computation.18 | async-start | bytes 3932160 | tf_op jit(solution)/shard_map/all_gather | solution.py:198
  224.9 266.1 %reduce-scatter.12.cloned.1.call-start = ((), (), s32[]{:S(2)}) async-start(), calls=%async_computation.17 | async-start | bytes 7864320 | tf_op jit(solution)/shard_map/reduce_scatter | solution.py:217
  381.5 173.2 %reduce-scatter.10.cloned.1.call-start = ((), (), s32[]{:S(2)}) async-start(), calls=%async_computation.16 | async-start | bytes 3932160 | tf_op jit(solution)/shard_map/reduce_scatter | solution.py:204
  390.5 450.3 %reduce-scatter.18.cloned.1.call-start = ((), (), s32[]{:S(2)}) async-start(), calls=%async_computation.21 | async-start | bytes 3538944 | tf_op jit(solution)/shard_map/reduce_scatter | solution.py:290
  397.6 8.8 copy-start.62
  397.6 443.3 %reduce-scatter.20.cloned.1.call-start = ((), (), s32[]{:S(2)}) async-start(), calls=%async_computation.22 | async-start | bytes 3538944 | tf_op jit(solution)/shard_map/reduce_scatter | solution.py:292
  493.6 65.4 %copy-start.28 = (bf16[1,512,768]{2,1,0:T(8,128)(2,1)S(1)}, bf16[1,512,768]{2,1,0:T(8,128)(2,1)}, u32[]{:S(2)}) copy-start(bf16[1,512,768]{2,1,0:T(8,128)(2,1)} %param.41) | copy-start | bytes 2359300
  562.0 14.4 %all-to-all-start.2 = ((bf16[512,4,192]{0,2,1:T(8,128)(2,1)}), bf16[512,4,192]{0,2,1:T(8,128)(2,1)S(1)}, u32[]{:S(2)}, u32[]{:S(2)}) async-start(bf16[512,4,192]{0,2,1:T(8,128)(2,1)} %bitcast.29), calls=%async_computation.4 | async-start | bytes 1572864 | tf_op jit(solution)/shard_map/all_to_all | solution.py:224
  565.6 275.8 %reduce-scatter.16.cloned.1.call-start = ((), (), s32[]{:S(2)}) async-start(), calls=%async_computation.20 | async-start | bytes 3538944 | tf_op jit(solution)/shard_map/reduce_scatter | solution.py:285
  569.0 8.9 copy-start.21
  569.1 282.6 %reduce-scatter.14.cloned.1.call-start = ((), (), s32[]{:S(2)}) async-start(), calls=%async_computation.19 | async-start | bytes 10616832 | tf_op jit(solution)/shard_map/reduce_scatter | solution.py:283
  578.0 60.4 %copy-start.12 = (bf16[2048,64]{1,0:T(8,128)(2,1)S(1)}, bf16[2048,64]{1,0:T(8,128)(2,1)}, u32[]{:S(2)}) copy-start(bf16[2048,64]{1,0:T(8,128)(2,1)} %copy-done.11) | copy-start | bytes 786436
  578.0 5.2 copy-start.31
  592.6 5.2 copy-start.31
  607.6 5.2 copy-start.31
  622.7 5.2 copy-start.31
  638.4 63.3 %copy-start.10 = (bf16[2048,64]{1,0:T(8,128)(2,1)S(1)}, bf16[2048,64]{1,0:T(8,128)(2,1)}, u32[]{:S(2)}) copy-start(bf16[2048,64]{1,0:T(8,128)(2,1)} %copy-done.9) | copy-start | bytes 786436
  723.0 5.0 copy-start.13
  723.0 5.0 copy-start.5
  736.9 5.0 copy-start.13
  736.9 5.0 copy-start.5
  750.8 5.0 copy-start.13
  757.2 5.2 copy-start.23
  757.2 7.4 copy-start.15
  823.1 7.0 copy-start.27
  823.1 7.0 copy-start.43
  823.1 7.0 copy-start.45
  823.1 7.0 copy-start.47
  823.1 7.0 copy-start.57
  837.1 41.0 %reduce-scatter.22.cloned.1.call-start = ((), (), s32[]{:S(2)}) async-start(), calls=%async_computation.23 | async-start | bytes 589824
  840.8 114.9 %all-reduce.16.cloned.1.call-start = ((), (), s32[]{:S(2)}) async-start(), calls=%async_computation.25 | async-start | bytes 4718592 | tf_op jit(solution)/shard_map/psum | solution.py:279
  840.9 10.8 copy-start.65
  840.9 12.1 %copy-start.29 = (bf16[1,512,768]{2,1,0:T(8,128)(2,1)S(1)}, bf16[1,512,768]{2,1,0:T(8,128)(2,1)}, u32[]{:S(2)}) copy-start(bf16[1,512,768]{2,1,0:T(8,128)(2,1)} %param.41) | copy-start | bytes 2359300
  841.4 287.2 %all-reduce.14.cloned.1.call-start = ((), (), s32[]{:S(2)}) async-start(), calls=%async_computation.24 | async-start | bytes 9437184 | tf_op jit(solution)/shard_map/psum | solution.py:265
  853.1 5.1 copy-start.49
  853.1 7.0 copy-start.52
  853.2 7.0 copy-start.53
  853.2 7.0 copy-start.54
  853.2 7.0 copy-start.55
  853.2 21.7 %copy-start.51 = (f32[512]{0:T(512)S(1)}, f32[512]{0:T(512)}, u32[]{:S(2)}) copy-start(f32[512]{0:T(512)} %copy-done.50) | copy-start | bytes 6148
  858.2 16.7 %copy-start.25 = (f32[512,768]{1,0:T(8,128)S(1)}, f32[512,768]{1,0:T(8,128)}, u32[]{:S(2)}) copy-start(f32[512,768]{1,0:T(8,128)} %copy-done.24) | copy-start | bytes 4718596
  1128.6 5.2 copy-start.37
  (69 other events, 170.7 us)
Sparse Core Ops, SparseCore 0:
  9.6 15.3 all-gather.14
  47.4 10.8 all-gather.16
  211.1 10.8 all-gather.20
  224.1 64.6 all-gather.18
  290.1 7.8 all-gather.22
  299.5 64.6 all-gather.24
  381.6 109.3 reduce-scatter.11
  493.9 60.7 reduce-scatter.9
  557.0 9.8 reduce-scatter.17
  569.1 11.0 reduce-scatter.19
  582.4 11.0 reduce-scatter.15
  837.2 14.4 reduce-scatter.13
  854.5 8.8 reduce-scatter.21
  866.7 76.0 all-reduce.15
  948.5 180.0 all-reduce.13
where the time goes:
time: 1150 us; the launch traced here: 1140 us
  waiting for transfers between devices  516 us (45%)
  matrix products  259 us (23%)
  blocking collectives  159 us (14%)
  local copies, waits for them, and re-layouts  125 us (11%)
  other arithmetic  37.8 us (3%)
  loops' own time  16.7 us (1%)
  between operations  16 us (1%)
  starting transfers between devices  13.8 us (1%)
    psum x1, waiting for transfers between devices, local(): lax.psum((grad_gain_one, grad_shift_one, grad_w_qkv, grad_qv_bias, grad_w...  173 us
    dot_general x40, matrix products, contract_last(): lax.dot_general(left, right, (((1,), (1,)), ((), ())), preferred_element_...  86.7 us
    reduce_scatter x1, waiting for transfers between devices, local(): lax.psum_scatter(grad_mlp_part, 'tensor', scatter_dimension=0, tiled=True)  82.8 us
    dot_general x28, matrix products, contract_first(): lax.dot_general(left, right, (((0,), (0,)), ((), ())), preferred_element_...  77.5 us
    psum x1, blocking collectives, local(): lax.psum((grad_gain_one, grad_shift_one, grad_w_qkv, grad_qv_bias, grad_w...  76.5 us
    all_gather x1, waiting for transfers between devices, local(): lax.all_gather(cot_rows, 'tensor', axis=0, tiled=True)  66.1 us
    all_gather x1, waiting for transfers between devices, local(): lax.all_gather(mlp_in, 'tensor', axis=0, tiled=True)  61.9 us
    reduce_scatter x1, waiting for transfers between devices, local(): lax.psum_scatter(partial_out.astype(jnp.bfloat16), 'tensor', scatter_dime...  61.1 us
  transfers between devices with their start and end apart: 18, of which 11 were waited for; matrix products, arithmetic and copies ran while one was open for 29% of the time, Pallas kernels for 0%

commit v1 on v0

v1 whole, which is shorter than its diff:
```python
import math

import jax
import jax.numpy as jnp
from jax import lax
from jax.experimental import pallas as pl
from jax.experimental.pallas import tpu as pltpu
from jax.sharding import PartitionSpec as P

HEAD_DIM = 64
BLOCK = 256
LONGEST = 1024
VMEM_BYTES = 48 * 1024 * 1024


EPSILON = 1e-05
NEGATIVE = -1e30


def layer_norm(values, gain, shift):
    center = jnp.mean(values, axis=-1, keepdims=True)
    offset = values - center
    spread = jnp.mean(offset * offset, axis=-1, keepdims=True)
    return offset * lax.rsqrt(spread + EPSILON) * gain + shift


def gelu_tanh(values):
    return jax.nn.gelu(values, approximate=True)


def contract_last(left, right):
    return lax.dot_general(
        left, right, (((1,), (1,)), ((), ())), preferred_element_type=jnp.float32
    )


def contract_first(left, right):
    return lax.dot_general(
        left, right, (((0,), (0,)), ((), ())), preferred_element_type=jnp.float32
    )


def sequence_starts(lengths, count):
    ends = jnp.cumsum(lengths)
    positions = jnp.arange(count, dtype=jnp.int32)
    past = ends[None, :] <= positions[:, None]
    return jnp.max(jnp.where(past, ends[None, :], 0), axis=1)


def window(number):
    start = number * BLOCK
    return start, max(0, start - LONGEST)


def block_scores(query, key_ref, first_ref, start, low):
    first = first_ref[start : start + BLOCK, 0:1]
    rows = lax.broadcasted_iota(jnp.int32, (BLOCK, BLOCK), 0)
    cols = lax.broadcasted_iota(jnp.int32, (BLOCK, BLOCK), 1)
    own = contract_last(query, key_ref[0, start : start + BLOCK, :])
    own = jnp.where((cols <= rows) & (cols >= first - start), own, NEGATIVE)
    if low == start:
        return own, None
    before = contract_last(query, key_ref[0, low:start, :])
    cols = lax.broadcasted_iota(jnp.int32, (BLOCK, start - low), 1)
    before = jnp.where(cols >= first - low, before, NEGATIVE)
    return own, before


def attend_kernel(first_ref, q_ref, k_ref, v_ref, out_ref, log_ref):
    group_len = q_ref.shape[1]
    for number in range(group_len // BLOCK):
        start, low = window(number)
        stop = start + BLOCK
        query = q_ref[0, start:stop, :]
        own, before = block_scores(query, k_ref, first_ref, start, low)
        largest = jnp.max(own, axis=1, keepdims=True)
        if before is not None:
            largest = jnp.maximum(largest, jnp.max(before, axis=1, keepdims=True))
        own = jnp.exp(own - largest)
        total = jnp.sum(own, axis=1, keepdims=True)
        if before is not None:
            before = jnp.exp(before - largest)
            total = total + jnp.sum(before, axis=1, keepdims=True)
        inverse = 1.0 / total
        result = jnp.dot(
            (own * inverse).astype(jnp.bfloat16),
            v_ref[0, start:stop, :],
            preferred_element_type=jnp.float32,
        )
        if before is not None:
            result = result + jnp.dot(
                (before * inverse).astype(jnp.bfloat16),
                v_ref[0, low:start, :],
                preferred_element_type=jnp.float32,
            )
        out_ref[0, start:stop, :] = result.astype(jnp.bfloat16)
        log_ref[0, start:stop, :] = jnp.broadcast_to(largest + jnp.log(total), (BLOCK, 128))


def attend_back_kernel(
    first_ref, q_ref, k_ref, v_ref, g_ref, log_ref, dq_ref, dk_ref, dv_ref, key_sum, value_sum
):
    group_len = q_ref.shape[1]
    scale = 1.0 / math.sqrt(HEAD_DIM)
    key_sum[...] = jnp.zeros_like(key_sum)
    value_sum[...] = jnp.zeros_like(value_sum)
    for number in range(group_len // BLOCK):
        start, low = window(number)
        stop = start + BLOCK
        query = q_ref[0, start:stop, :]
        grad = g_ref[0, start:stop, :]
        log_total = log_ref[0, start:stop, 0:1]
        scores = block_scores(query, k_ref, first_ref, start, low)
        parts = []
        weighted = None
        for part, begin, end in ((scores[0], start, stop), (scores[1], low, start)):
            if part is None:
                continue
            probs = jnp.exp(part - log_total)
            grad_probs = contract_last(grad, v_ref[0, begin:end, :])
            term = jnp.sum(probs * grad_probs, axis=1, keepdims=True)
            weighted = term if weighted is None else weighted + term
            parts.append((probs, grad_probs, begin, end))
        grad_query = None
        for probs, grad_probs, begin, end in parts:
            grad_scores = (probs * (grad_probs - weighted)).astype(jnp.bfloat16)
            term = jnp.dot(grad_scores, k_ref[0, begin:end, :], preferred_element_type=jnp.float32)
            grad_query = term if grad_query is None else grad_query + term
            key_sum[begin:end, :] += contract_first(grad_scores, query)
            value_sum[begin:end, :] += contract_first(probs.astype(jnp.bfloat16), grad)
        dq_ref[0, start:stop, :] = (grad_query * scale).astype(jnp.bfloat16)
    dk_ref[0] = key_sum[...].astype(jnp.bfloat16)
    dv_ref[0] = value_sum[...].astype(jnp.bfloat16)


def head_spec(group_len, width, offset=0):
    return pl.BlockSpec((1, group_len, width), lambda head: (head + offset, 0, 0))


def attend(first, heads_in):
    head_count, group_len, width = heads_in.shape
    head_count = head_count // 3
    return pl.pallas_call(
        attend_kernel,
        grid=(head_count,),
        in_specs=[pl.BlockSpec((group_len, 128), lambda head: (0, 0))]
        + [head_spec(group_len, width, head_count * part) for part in range(3)],
        out_specs=[head_spec(group_len, width), head_spec(group_len, 128)],
        out_shape=[
            jax.ShapeDtypeStruct((head_count, group_len, width), jnp.bfloat16),
            jax.ShapeDtypeStruct((head_count, group_len, 128), jnp.float32),
        ],
        compiler_params=pltpu.CompilerParams(vmem_limit_bytes=VMEM_BYTES),
        cost_estimate=pl.CostEstimate(
            flops=head_count * group_len * 1280 * 256,
            bytes_accessed=head_count * group_len * 1536,
            transcendentals=head_count * group_len * 1280,
        ),
    )(first, heads_in, heads_in, heads_in)


def attend_back(first, heads_in, grad_out, log_total):
    head_count, group_len, width = grad_out.shape
    like = jax.ShapeDtypeStruct((head_count, group_len, width), jnp.bfloat16)
    return pl.pallas_call(
        attend_back_kernel,
        grid=(head_count,),
        in_specs=[pl.BlockSpec((group_len, 128), lambda head: (0, 0))]
        + [head_spec(group_len, width, head_count * part) for part in range(3)]
        + [head_spec(group_len, width), head_spec(group_len, 128)],
        out_specs=[head_spec(group_len, width)] * 3,
        out_shape=[like] * 3,
        scratch_shapes=[pltpu.VMEM((group_len, width), jnp.float32)] * 2,
        compiler_params=pltpu.CompilerParams(vmem_limit_bytes=VMEM_BYTES),
        cost_estimate=pl.CostEstimate(
            flops=head_count * group_len * 1280 * 640,
            bytes_accessed=head_count * group_len * 2048,
            transcendentals=head_count * group_len * 1280,
        ),
    )(first, heads_in, heads_in, heads_in, grad_out, log_total)


def gather(values, axis_name, axis=0):
    return lax.all_gather(values, axis_name, axis=axis, tiled=True)


def scatter_sum(values, axis_name, axis=0):
    return lax.psum_scatter(values, axis_name, scatter_dimension=axis, tiled=True)


def local(
    tokens,
    ln1_gain,
    ln1_bias,
    w_qkv,
    bias_qv,
    w_out,
    bias_out,
    ln2_gain,
    ln2_bias,
    w_in,
    bias_in,
    w_back,
    bias_back,
    seq_lengths,
    cotangent,
):
    low, full = jnp.bfloat16, jnp.float32
    tok_count, width = tokens.shape[1], tokens.shape[2]
    parts = lax.axis_size("heads")
    mine = lax.axis_index("heads")
    part_width = width // parts
    head_count = part_width // HEAD_DIM
    shard_rows = w_qkv.shape[0]

    group_tokens = gather(tokens[0], "heads")
    group_len = group_tokens.shape[0]
    own_qkv = lax.dynamic_slice_in_dim(
        w_qkv.reshape(shard_rows, 3, width), mine * part_width, part_width, 2
    ).reshape(shard_rows, 3 * part_width)
    own_qkv = gather(own_qkv, "shard")
    vectors = gather(
        jnp.concatenate(
            [
                jnp.stack([ln1_gain, ln1_bias, bias_out, ln2_gain, ln2_bias, bias_back]),
                bias_qv,
            ]
        ),
        "shard",
        1,
    ).astype(full)
    gain_one, shift_one, out_bias, gain_two, shift_two, back_bias = (vectors[i] for i in range(6))
    full_out = gather(w_out, "shard")
    full_in = gather(gather(w_in, "tensor"), "shard")
    full_back = gather(gather(w_back, "tensor"), "shard")
    in_bias = gather(gather(bias_in, "tensor"), "shard").astype(full)

    inputs = tokens[0].astype(full)
    _, norm_one_back = jax.vjp(layer_norm, inputs, gain_one, shift_one)
    attn_in = layer_norm(group_tokens.astype(full), gain_one, shift_one).astype(low)
    own_bias = lax.dynamic_slice_in_dim(vectors[6:8], mine * part_width, part_width, 1)
    qkv_bias = jnp.concatenate([own_bias[0], jnp.zeros((part_width,), full), own_bias[1]])
    projected = (jnp.dot(attn_in, own_qkv, preferred_element_type=full) + qkv_bias).astype(low)
    shrink = jnp.where(jnp.arange(3 * part_width) < part_width, 1.0 / math.sqrt(HEAD_DIM), 1.0)
    heads_in = (
        (projected * shrink.astype(low))
        .reshape(group_len, 3 * head_count, HEAD_DIM)
        .transpose(1, 0, 2)
    )
    first = jnp.broadcast_to(
        sequence_starts(seq_lengths[0], group_len)[:, None], (group_len, 128)
    )
    attended, log_total = attend(first, heads_in)
    attended = attended.transpose(1, 0, 2).reshape(group_len, part_width)
    back_tok = lax.all_to_all(attended, "heads", split_axis=0, concat_axis=1, tiled=True)
    hidden_res = inputs + jnp.dot(back_tok, full_out, preferred_element_type=full) + out_bias

    normed_two, norm_two_back = jax.vjp(layer_norm, hidden_res, gain_two, shift_two)
    mlp_in = normed_two.astype(low)
    cot_rows = cotangent[0]
    cot_float = cot_rows.astype(full)
    pre_act = contract_last(mlp_in, full_in) + in_bias
    activated, gelu_back = jax.vjp(gelu_tanh, pre_act)
    act_low = activated.astype(low)
    branch = jnp.dot(act_low, full_back, preferred_element_type=full)
    output = (hidden_res + branch + back_bias).astype(low)[None]
    grad_w_back = contract_first(act_low, cot_rows).astype(low)
    grad_act = contract_last(cot_rows, full_back)
    grad_pre = gelu_back(grad_act)[0].astype(low)
    grad_in_bias = jnp.sum(grad_pre.astype(full), axis=0)
    grad_w_in = contract_first(grad_pre, mlp_in).astype(low)
    grad_normed_two = jnp.dot(grad_pre, full_in, preferred_element_type=full)
    grad_res_norm, grad_gain_two, grad_shift_two = norm_two_back(grad_normed_two)
    grad_hidden = cot_float + grad_res_norm
    hidden_low = grad_hidden.astype(low)
    grad_w_out = contract_first(back_tok, hidden_low).astype(low)

    grad_attended = contract_last(hidden_low, full_out).astype(low)
    grad_heads = lax.all_to_all(grad_attended, "heads", split_axis=1, concat_axis=0, tiled=True)
    grad_heads = grad_heads.reshape(group_len, head_count, HEAD_DIM).transpose(1, 0, 2)
    grads = attend_back(first, heads_in, grad_heads, log_total)
    grad_proj = (
        jnp.concatenate(grads, axis=0).transpose(1, 0, 2).reshape(group_len, 3 * part_width)
    )
    grad_attn_in = scatter_sum(contract_last(grad_proj, own_qkv).astype(low), "heads").astype(full)
    grad_w_qkv = contract_first(attn_in, grad_proj).astype(low)
    grad_proj_sum = jnp.sum(grad_proj.astype(full), axis=0).reshape(3, part_width)
    grad_qv_bias = lax.dynamic_update_slice_in_dim(
        jnp.zeros((2, width), full), grad_proj_sum[0::2], mine * part_width, 1
    )
    grad_input_norm, grad_gain_one, grad_shift_one = norm_one_back(grad_attn_in)
    input_grad = (grad_hidden + grad_input_norm).astype(low)[None]

    own_back = lax.psum(scatter_sum(scatter_sum(grad_w_back, "shard"), "tensor"), "heads")
    own_in = lax.psum(scatter_sum(scatter_sum(grad_w_in, "shard"), "tensor"), "heads")
    own_out = lax.psum(scatter_sum(grad_w_out, "shard"), ("heads", "tensor"))
    part_qkv = lax.psum(scatter_sum(grad_w_qkv, "shard"), "tensor")
    own_grad_qkv = (
        lax.all_gather(part_qkv.reshape(shard_rows, 3, part_width), "heads", axis=2, tiled=True)
        .reshape(shard_rows, 3 * width)
        .astype(full)
    )
    sums = lax.psum(
        jnp.concatenate(
            [
                jnp.stack(
                    [
                        grad_gain_one,
                        grad_shift_one,
                        jnp.sum(hidden_low.astype(full), axis=0),
                        grad_gain_two,
                        grad_shift_two,
                        jnp.sum(cot_float, axis=0),
                    ]
                ),
                grad_qv_bias,
                grad_in_bias.reshape(-1, width),
            ]
        ),
        ("shard", "heads", "tensor"),
    )
    shard = lax.axis_index("shard")
    owned = lax.dynamic_slice_in_dim(sums[:8], shard * shard_rows, shard_rows, 1)
    hidden_rows = bias_in.shape[0]
    place = shard * lax.axis_size("tensor") + lax.axis_index("tensor")
    own_in_bias = lax.dynamic_slice_in_dim(
        sums[8:].reshape(-1), place * hidden_rows, hidden_rows, 0
    )
    return (
        output,
        input_grad,
        owned[0],
        owned[1],
        own_grad_qkv,
        owned[6:8],
        own_out.astype(full),
        owned[2],
        owned[3],
        owned[4],
        own_in.astype(full),
        own_in_bias,
        own_back.astype(full),
        owned[5],
    )


def solution(mesh):
    in_specs = (
        P(("shard", "tensor"), "heads", None),
        P("shard"),
        P("shard"),
        P("shard", None),
        P(None, "shard"),
        P("shard", None),
        P("shard"),
        P("shard"),
        P("shard"),
        P(("shard", "tensor"), None),
        P(("shard", "tensor")),
        P(("shard", "tensor"), None),
        P("shard"),
        P(("shard", "tensor"), None),
        P(("shard", "tensor"), "heads", None),
    )
    out_specs = (
        P(("shard", "tensor"), "heads", None),
        P(("shard", "tensor"), "heads", None),
        P("shard"),
        P("shard"),
        P("shard", None),
        P(None, "shard"),
        P("shard", None),
        P("shard"),
        P("shard"),
        P("shard"),
        P(("shard", "tensor"), None),
        P(("shard", "tensor")),
        P(("shard", "tensor"), None),
        P("shard"),
    )
    return jax.shard_map(local, mesh=mesh, in_specs=in_specs, out_specs=out_specs, check_vma=False)
```

time: 1150 us -> 775 us (0.67)
  matrix products: 259 us -> 66.1 us
  blocking collectives: 159 us -> 74.3 us
  local copies, waits for them, and re-layouts: 125 us -> 42.8 us
  Pallas kernels: 0 us -> 45.5 us
  waiting for transfers between devices: 516 us -> 492 us
  loops' own time: 16.7 us -> 0 us
  other arithmetic: 37.8 us -> 25.6 us
    dot_general x28 -> x4, matrix products: 94.8 us -> 17.5 us  [the longest x1 9.46 us: local(): branch = jnp.dot(act_low, full_back, preferred_element_type=full)]
    dot_general x40 -> x4, matrix products: 86.7 us -> 24.5 us  [contract_last(): lax.dot_general(left, right, (((1,), (1,)), ((), ())), preferred_element_...]
    while x137 -> x0, local copies, waits for them, and re-layouts: 56.2 us -> none
    dot_general x28 -> x4, matrix products: 77.5 us -> 24.2 us  [contract_first(): lax.dot_general(left, right, (((0,), (0,)), ((), ())), preferred_element_...]
    psum x2 -> x1, blocking collectives: 87.3 us -> 39.9 us  [local(): lax.psum(jnp.concatenate([jnp.stack([grad_gain_one, grad_shift_one, jnp.s...]
    pallas_call x0 -> x2, Pallas kernels: none -> 45.5 us  [the longest x1 27.6 us: attend_back(): pl.pallas_call(attend_back_kernel, grid=(head_count,), in_specs=[pl.Block...]
    all_to_all x2 -> x0, waiting for transfers between devices: 42.9 us -> none  [the longest x1 35.9 us: local(): lax.all_to_all(projected.reshape(tok_count, 3, width), 'heads', split_axi...]
    all_to_all x1, blocking collectives: 53.2 us -> 15.9 us  [local(): lax.all_to_all(grad_attended, 'heads', split_axis=1, concat_axis=0, tiled...]
  transfers between devices with their start and end apart: 18 -> 18, of which waited for: 11 -> 13; matrix products, arithmetic and copies ran while one was open for 29% -> 11% of each run, Pallas kernels for 0% -> 2%
where the time goes in v1:
time: 775 us; the launch traced here: 766 us
  waiting for transfers between devices  492 us (63%)
  blocking collectives  74.3 us (10%)
  matrix products  66.1 us (9%)
  Pallas kernels  45.5 us (6%)
  local copies, waits for them, and re-layouts  42.8 us (6%)
  other arithmetic  25.6 us (3%)
  between operations  15 us (2%)
    reduce_scatter x6, waiting for transfers between devices, scatter_sum(): lax.psum_scatter(values, axis_name, scatter_dimension=axis, tiled=True)  168 us
    all_gather x6, waiting for transfers between devices, gather(): return lax.all_gather(values, axis_name, axis=axis, tiled=True)  140 us
    psum x1, waiting for transfers between devices, local(): own_out = lax.psum(scatter_sum(grad_w_out, 'shard'), ('heads', 'tensor'))  100 us
    psum x1, blocking collectives, local(): lax.psum(jnp.concatenate([jnp.stack([grad_gain_one, grad_shift_one, jnp.s...  39.9 us
    psum x1, waiting for transfers between devices, local(): part_qkv = lax.psum(scatter_sum(grad_w_qkv, 'shard'), 'tensor')  34.3 us
    all_gather x1, waiting for transfers between devices, local(): lax.all_gather(part_qkv.reshape(shard_rows, 3, part_width), 'heads', axis...  31.3 us
    pallas_call x1, Pallas kernels, attend_back(): pl.pallas_call(attend_back_kernel, grid=(head_count,), in_specs=[pl.Block...  27.6 us
    dot_general x4, matrix products, contract_last(): lax.dot_general(left, right, (((1,), (1,)), ((), ())), preferred_element_...  24.5 us
  transfers between devices with their start and end apart: 18, of which 13 were waited for; matrix products, arithmetic and copies ran while one was open for 11% of the time, Pallas kernels for 2%

profile of v1, /device:TPU:0, one launch (start us, length us, event | category | flops | bytes accessed | tf_op | source)
XLA Modules:
  0.0 765.6 jit_solution(4355091186234157380)
XLA Ops:
  8.0 0.7 all-gather.17.cloned.1.call-update
  10.1 52.8 %all-gather.13.cloned.1.call-done = bf16[1536,768]{1,0:T(8,128)(2,1)} async-done(((bf16[384,768]{1,0:T(8,128)(2,1)}), bf16[1536,768]{1,0:T(8,128)(2,1)}) %all-gather.13.cloned.1.call-update) | async-done | bytes 2359312 | tf_op jit(solution)/shard_map/all_gather | solution.py:184
  63.1 1.8 all_gather.34
  64.9 2.8 copy.48
  68.1 45.7 %all-gather.17.cloned.1.call-done = bf16[1536,768]{1,0:T(8,128)(2,1)} async-done(((bf16[384,768]{1,0:T(8,128)(2,1)}), bf16[1536,768]{1,0:T(8,128)(2,1)}) %all-gather.17.cloned.1.call-update) | async-done | bytes 2359312 | tf_op jit(solution)/shard_map/all_gather | solution.py:184
  114.0 2.4 all_gather.35
  116.4 42.0 %all-gather.23.cloned.1.call-done = bf16[1,2048,768]{2,1,0:T(8,128)(2,1)} async-done(((bf16[1,512,768]{2,1,0:T(8,128)(2,1)}), bf16[1,2048,768]{2,1,0:T(8,128)(2,1)}) %all-gather.23.cloned.1.call-update) | async-done | bytes 3145744 | tf_op jit(solution)/shard_map/all_gather | solution.py:184
  158.4 2.5 convert_reduce_fusion.1
  161.3 1.1 fusion.3
  162.4 2.6 fusion.14
  165.0 4.0 copy.49
  169.3 17.9 %shard_map.254 = (bf16[3,2048,64]{2,1,0:T(8,128)(2,1)S(1)}, f32[3,2048,128]{2,1,0:T(8,128)S(1)}) custom-call(s32[2048,128]{1,0:T(8,128)S(1)} %broadcast_in_dim.61.first_ref, bf16[9,2048,64]{2,1,0:T(8,128)(2,1)} %bitcast.116, bf16[9,2048,64]{2,1,0:T(8,128)(2,1)} %bitcast.117, bf16[9,2048,64]{2,1,0:T(8,128)(2,1)} %bitcast.118), custom_call_target="tpu_custom_call" | custom-call | flops 2013265920 | bytes 9437184 | tf_op jit(solution)/shard_map/pallas_call | solution.py:143
  187.3 1.7 copy-done
  188.9 1.4 copy.50
  190.3 2.3 all_to_all.26
  192.6 1.0 copy.51
  193.6 3.5 all-to-all-start
  197.2 11.9 %all-gather.1 = bf16[4,1,384]{2,1,0:T(2,128)(2,1)S(1)} all-gather(bf16[1,1,384]{2,1,0:T(2,128)(2,1)S(1)} %reshape.201), channel_id=1, replica_groups=mesh['shard'=2,'heads'=4,'tensor'=4] {'tensor'}, dimensions={0}, use_global_device_ids=true | all-gather | bytes 3840 | tf_op jit(solution)/shard_map/all_gather | solution.py:184
  209.1 2.3 all-gather.2
  211.5 0.9 copy-done.8
  212.3 2.4 fusion.42
  215.1 7.3 fusion.37
  222.5 9.2 %convert_reduce_fusion.2 = (f32[3072]{0:T(1024)S(1)}, bf16[512,3072]{1,0:T(8,128)(2,1)S(1)}) fusion(f32[512,3072]{1,0:T(8,128)} %fusion.37, f32[3072]{0:T(1024)S(1)} %bitcast.134, bf16[3072,768]{1,0:T(8,128)(2,1)} %all-gather.19.cloned.1.call-done, bf16[1,512,768]{2,1,0:T(8,128)(2,1)} %param.29), kind=kOutput, calls=%fused_computation.19 | convolution fusion | flops 2452091904 | bytes 14966784 | tf_op jit(solution)/shard_map/dot_general | solution.py:32
  231.7 2.9 multiply_reduce_fusion
  234.7 2.1 fusion.41
  237.2 0.9 copy-done.9
  238.1 1.7 convolution_convert_fusion.5
  239.8 2.3 copy.52
  242.1 15.9 %all_to_all.35 = bf16[512,4,192]{0,2,1:T(8,128)(2,1)S(1)} all-to-all(bf16[512,4,192]{0,2,1:T(8,128)(2,1)} %bitcast.123), channel_id=1, replica_groups=mesh['shard'=2,'heads'=4,'tensor'=4] {'heads'}, dimensions={1} | all-to-all | bytes 1572864 | tf_op jit(solution)/shard_map/all_to_all | solution.py:279
  258.0 1.5 copy.53
  259.5 2.8 reshape.187
  262.3 2.5 copy.54
  264.8 27.6 %shard_map.255 = (bf16[3,2048,64]{2,1,0:T(8,128)(2,1)S(1)}, bf16[3,2048,64]{2,1,0:T(8,128)(2,1)S(1)}, bf16[3,2048,64]{2,1,0:T(8,128)(2,1)S(1)}) custom-call(s32[2048,128]{1,0:T(8,128)S(1)} %broadcast_in_dim.61.first_ref, bf16[9,2048,64]{2,1,0:T(8,128)(2,1)} %bitcast.119, bf16[9,2048,64]{2,1,0:T(8,128)(2,1)} %bitcast.120, bf16[9,2048,64]{2,1,0:T(8,128)(2,1)} %bitcast.121, ...), custom_call_target="tpu_custom_call" | custom-call | flops 5033164800 | bytes 12582912 | tf_op jit(solution)/shard_map/pallas_call | solution.py:165
  292.3 3.0 convert_reduce_fusion
  295.3 6.0 copy.55
  301.3 4.9 convolution_convert_fusion.4
  306.2 1.3 copy.57
  307.6 3.2 convolution_convert_fusion.3
  310.8 3.5 reduce-scatter.22.cloned.1.call-done
  314.4 2.0 copy.58
  316.4 7.4 convolution_convert_fusion.1
  323.8 1.1 copy-done.6
  325.0 8.8 %convolution_convert_fusion = bf16[3072,768]{1,0:T(8,128)(2,1)} fusion(bf16[1,512,768]{2,1,0:T(8,128)(2,1)S(1)} %copy-done.6, f32[512,3072]{1,0:T(8,128)} %fusion.37, f32[3072]{0:T(1024)S(1)} %bitcast.135), kind=kOutput, calls=%fused_computation.21 | convolution fusion | flops 2434007040 | bytes 11808768 | tf_op jit(solution)/shard_map/dot_general | solution.py:38
  334.4 34.3 %all-reduce.5.cloned.1.call-done = bf16[384,3,192]{0,2,1:T(8,128)(2,1)} async-done(((bf16[384,3,192]{0,2,1:T(8,128)(2,1)}), bf16[384,3,192]{0,2,1:T(8,128)(2,1)}) %all-reduce.5.cloned.1.call-update) | async-done | bytes 442384 | tf_op jit(solution)/shard_map/psum | solution.py:297
  368.7 14.8 %reduce-scatter.14.cloned.1.call-done = bf16[1536,768]{1,0:T(8,128)(2,1)} async-done(((bf16[3072,768]{1,0:T(8,128)(2,1)}), bf16[1536,768]{1,0:T(8,128)(2,1)}) %reduce-scatter.14.cloned.1.call-update) | async-done | bytes 2359312 | tf_op jit(solution)/shard_map/reduce_scatter | solution.py:188
  383.6 16.0 %reduce-scatter.18.cloned.1.call-done = bf16[1536,768]{1,0:T(8,128)(2,1)} async-done(((bf16[3072,768]{1,0:T(8,128)(2,1)}), bf16[1536,768]{1,0:T(8,128)(2,1)}) %reduce-scatter.18.cloned.1.call-update) | async-done | bytes 2359312 | tf_op jit(solution)/shard_map/reduce_scatter | solution.py:188
  399.9 6.3 convolution_convert_fusion.2
  406.6 9.5 %fusion.26 = bf16[1,512,768]{2,1,0:T(8,128)(2,1)} fusion(f32[512,768]{1,0:T(8,128)} %copy-done.4, bf16[3072,768]{1,0:T(8,128)(2,1)} %all-gather.19.cloned.1.call-done, f32[768]{0:T(1024)S(1)} %get-tuple-element.81, f32[512,3072]{1,0:T(8,128)} %fusion.37, f32[3072]{0:T(1024)S(1)} %bitcast.136), kind=kOutput, calls=%fused_computation.58 | convolution fusion | flops 2432827392 | bytes 13384704 | tf_op jit(solution)/shard_map/dot_general | solution.py:265
  416.3 100.0 %all-reduce.7.cloned.1.call-done = bf16[384,768]{1,0:T(8,128)(2,1)} async-done(((bf16[384,768]{1,0:T(8,128)(2,1)}), bf16[384,768]{1,0:T(8,128)(2,1)}) %all-reduce.7.cloned.1.call-update) | async-done | bytes 589840 | tf_op jit(solution)/shard_map/psum | solution.py:296
  516.3 2.2 convert_element_type.116
  518.5 31.3 %all-gather.21.cloned.1.call-done = bf16[384,3,768]{0,2,1:T(8,128)(2,1)} async-done(((bf16[384,3,192]{0,2,1:T(8,128)(2,1)}), bf16[384,3,768]{0,2,1:T(8,128)(2,1)}) %all-gather.21.cloned.1.call-update) | async-done | bytes 1769488 | tf_op jit(solution)/shard_map/all_gather | solution.py:299
  549.8 3.5 bitcast_convert_fusion
  553.2 5.2 copy.56
  558.4 41.6 %reduce-scatter.16.cloned.1.call-done = bf16[384,768]{1,0:T(8,128)(2,1)} async-done(((bf16[1536,768]{1,0:T(8,128)(2,1)}), bf16[384,768]{1,0:T(8,128)(2,1)}) %reduce-scatter.16.cloned.1.call-update) | async-done | bytes 589840 | tf_op jit(solution)/shard_map/reduce_scatter | solution.py:188
  600.0 49.7 %reduce-scatter.20.cloned.1.call-done = bf16[384,768]{1,0:T(8,128)(2,1)} async-done(((bf16[1536,768]{1,0:T(8,128)(2,1)}), bf16[384,768]{1,0:T(8,128)(2,1)}) %reduce-scatter.20.cloned.1.call-update) | async-done | bytes 589840 | tf_op jit(solution)/shard_map/reduce_scatter | solution.py:188
  649.7 46.3 %reduce-scatter.10.cloned.1.call-done = bf16[512,768]{1,0:T(8,128)(2,1)} async-done(((bf16[2048,768]{1,0:T(8,128)(2,1)}), bf16[512,768]{1,0:T(8,128)(2,1)}) %reduce-scatter.10.cloned.1.call-update) | async-done | bytes 786448 | tf_op jit(solution)/shard_map/reduce_scatter | solution.py:188
  696.1 1.9 fusion.22
  698.0 2.1 fusion.25
  700.1 1.7 convert_reduce_fusion.5
  701.9 39.9 %psum.35 = f32[12,768]{1,0:T(8,128)S(1)} all-reduce(f32[12,768]{1,0:T(8,128)S(1)} %concatenate.15), channel_id=1, replica_groups=mesh['shard'=2,'heads'=4,'tensor'=4] {'shard','heads','tensor'}, use_global_device_ids=true, to_apply=%region_21.22 | all-reduce | flops 9216 | bytes 73728 | tf_op jit(solution)/shard_map/psum | solution.py:303
  743.1 0.7 dynamic-slice_reduce_fusion
  743.8 10.5 %all-reduce.9.cloned.1.call-done = (bf16[384,768]{1,0:T(8,128)(2,1)}, bf16[384,768]{1,0:T(8,128)(2,1)}) async-done(((bf16[384,768]{1,0:T(8,128)(2,1)}, bf16[384,768]{1,0:T(8,128)(2,1)}), (bf16[384,768]{1,0:T(8,128)(2,1)}, bf16[384,768]{1,0:T(8,128)(2,1)})) %all-reduce.9.cloned.1.call-update) | async-done | bytes 1179664 | tf_op jit(solution)/shard_map/psum | solution.py:295
  754.3 2.2 convert_element_type.118
  756.5 2.2 convert_element_type.120
  (126 shorter events, 7.4 us)
Async XLA Ops:
  7.2 55.8 %copy-start.11 = (bf16[384]{0:T(512)(128)(2,1)S(1)}, bf16[384]{0:T(512)(128)(2,1)}, u32[]{:S(2)}) copy-start(bf16[384]{0:T(512)(128)(2,1)} %param.16) | copy-start | bytes 2308
  7.2 55.8 %copy-start.12 = (bf16[384]{0:T(512)(128)(2,1)S(1)}, bf16[384]{0:T(512)(128)(2,1)}, u32[]{:S(2)}) copy-start(bf16[384]{0:T(512)(128)(2,1)} %param.17) | copy-start | bytes 2308
  7.2 55.8 %copy-start.13 = (bf16[384]{0:T(512)(128)(2,1)S(1)}, bf16[384]{0:T(512)(128)(2,1)}, u32[]{:S(2)}) copy-start(bf16[384]{0:T(512)(128)(2,1)} %param.21) | copy-start | bytes 2308
  7.2 55.8 %copy-start.14 = (bf16[384]{0:T(512)(128)(2,1)S(1)}, bf16[384]{0:T(512)(128)(2,1)}, u32[]{:S(2)}) copy-start(bf16[384]{0:T(512)(128)(2,1)} %param.22) | copy-start | bytes 2308
  7.2 55.8 %copy-start.15 = (bf16[384]{0:T(512)(128)(2,1)S(1)}, bf16[384]{0:T(512)(128)(2,1)}, u32[]{:S(2)}) copy-start(bf16[384]{0:T(512)(128)(2,1)} %param.23) | copy-start | bytes 2308
  7.2 55.8 %copy-start.16 = (bf16[384]{0:T(512)(128)(2,1)S(1)}, bf16[384]{0:T(512)(128)(2,1)}, u32[]{:S(2)}) copy-start(bf16[384]{0:T(512)(128)(2,1)} %param.27) | copy-start | bytes 2308
  7.2 55.8 %copy-start.10 = (bf16[2,384]{1,0:T(2,128)(2,1)S(1)}, bf16[2,384]{1,0:T(2,128)(2,1)}, u32[]{:S(2)}) copy-start(bf16[2,384]{1,0:T(2,128)(2,1)} %param.19) | copy-start | bytes 4612
  7.3 55.6 %all-gather.13.cloned.1.call-start = ((), (), s32[]{:S(2)}) async-start(), calls=%async_computation.10 | async-start | bytes 2949120 | tf_op jit(solution)/shard_map/all_gather | solution.py:184
  8.0 105.8 %all-gather.17.cloned.1.call-start = ((), (), s32[]{:S(2)}) async-start(), calls=%async_computation.12 | async-start | bytes 2949120 | tf_op jit(solution)/shard_map/all_gather | solution.py:184
  8.7 149.7 %all-gather.23.cloned.1.call-start = ((), (), s32[]{:S(2)}) async-start(), calls=%async_computation.23 | async-start | bytes 3932160 | tf_op jit(solution)/shard_map/all_gather | solution.py:184
  9.5 202.0 %all-gather.11.cloned.1.call-start = ((), (), s32[]{:S(2)}) async-start(), calls=%async_computation.9 | async-start | bytes 1769472 | tf_op jit(solution)/shard_map/all_gather | solution.py:184
  10.0 57.7 %copy-start.20 = (s32[1,4]{1,0:T(1,128)S(1)}, s32[1,4]{1,0:T(1,128)}, u32[]{:S(2)}) copy-start(s32[1,4]{1,0:T(1,128)} %param.28) | copy-start | bytes 52
  10.1 205.1 %all-gather.15.cloned.1.call-start = ((), (), s32[]{:S(2)}) async-start(), calls=%async_computation.11 | async-start | bytes 7077888 | tf_op jit(solution)/shard_map/all_gather | solution.py:184
  62.9 159.6 %all-gather.19.cloned.1.call-start = ((), (), s32[]{:S(2)}) async-start(), calls=%async_computation.13 | async-start | bytes 7077888 | tf_op jit(solution)/shard_map/all_gather | solution.py:184
  116.4 45.9 %copy-start.7 = (bf16[768,576]{0,1:T(8,128)(2,1)}, bf16[768,576]{0,1:T(8,128)(2,1)S(1)}, u32[]{:S(2)}) copy-start(bf16[768,576]{0,1:T(8,128)(2,1)S(1)} %all_gather.35) | copy-start | bytes 2654212
  158.4 2.8 copy-start.2
  187.2 1.7 copy-start
  188.9 8.3 %copy-start.17 = (bf16[384]{0:T(512)(128)(2,1)S(1)}, bf16[384]{0:T(512)(128)(2,1)}, u32[]{:S(2)}) copy-start(bf16[384]{0:T(512)(128)(2,1)} %param.25) | copy-start | bytes 2308
  188.9 23.4 %copy-start.1 = (bf16[1,512,768]{2,1,0:T(8,128)(2,1)S(1)}, bf16[1,512,768]{2,1,0:T(8,128)(2,1)}, u32[]{:S(2)}) copy-start(bf16[1,512,768]{2,1,0:T(8,128)(2,1)} %param.15) | copy-start | bytes 2359300
  193.6 17.8 %all-to-all-start = ((bf16[4,512,192]{1,2,0:T(8,128)(2,1)}), bf16[4,512,192]{1,2,0:T(8,128)(2,1)S(1)}, u32[]{:S(2)}, u32[]{:S(2)}) async-start(bf16[4,512,192]{1,2,0:T(8,128)(2,1)} %copy.51), calls=%async_computation | async-start | bytes 1572864 | tf_op jit(solution)/shard_map/all_to_all | solution.py:255
  197.2 117.2 %reduce-scatter.22.cloned.1.call-start = ((), (), s32[]{:S(2)}) async-start(), calls=%async_computation.24 | async-start | bytes 1474560
  211.5 0.9 copy-start.8
  214.8 16.9 %copy-start.4 = (f32[512,768]{1,0:T(8,128)}, f32[512,768]{1,0:T(8,128)S(1)}, u32[]{:S(2)}) copy-start(f32[512,768]{1,0:T(8,128)S(1)} %get-tuple-element.101) | copy-start | bytes 4718596
  222.5 9.3 %copy-start.18 = (bf16[3072,768]{1,0:T(8,128)(2,1)S(1)}, bf16[3072,768]{1,0:T(8,128)(2,1)}, u32[]{:S(2)}) copy-start(bf16[3072,768]{1,0:T(8,128)(2,1)} %all-gather.15.cloned.1.call-done) | copy-start | bytes 14155780
  231.7 3.0 copy-start.21
  234.7 2.2 copy-start.5
  234.7 3.4 copy-start.19
  237.2 0.9 copy-start.9
  307.5 26.3 %reduce-scatter.12.cloned.1.call-start = ((), (), s32[]{:S(2)}) async-start(), calls=%async_computation.17 | async-start | bytes 1769472 | tf_op jit(solution)/shard_map/reduce_scatter | solution.py:188
  310.8 57.9 %all-reduce.5.cloned.1.call-start = ((), (), s32[]{:S(2)}) async-start(), calls=%async_computation.15 | async-start | bytes 884736 | tf_op jit(solution)/shard_map/psum | solution.py:297
  316.4 67.2 %reduce-scatter.14.cloned.1.call-start = ((), (), s32[]{:S(2)}) async-start(), calls=%async_computation.19 | async-start | bytes 7077888 | tf_op jit(solution)/shard_map/reduce_scatter | solution.py:188
  323.8 1.2 copy-start.6
  323.8 75.8 %reduce-scatter.18.cloned.1.call-start = ((), (), s32[]{:S(2)}) async-start(), calls=%async_computation.21 | async-start | bytes 7077888 | tf_op jit(solution)/shard_map/reduce_scatter | solution.py:188
  333.8 182.6 %all-reduce.7.cloned.1.call-start = ((), (), s32[]{:S(2)}) async-start(), calls=%async_computation.18 | async-start | bytes 1179648 | tf_op jit(solution)/shard_map/psum | solution.py:296
  334.3 215.4 %all-gather.21.cloned.1.call-start = ((), (), s32[]{:S(2)}) async-start(), calls=%async_computation.16 | async-start | bytes 2211840 | tf_op jit(solution)/shard_map/all_gather | solution.py:299
  368.7 231.3 %reduce-scatter.16.cloned.1.call-start = ((), (), s32[]{:S(2)}) async-start(), calls=%async_computation.20 | async-start | bytes 2949120 | tf_op jit(solution)/shard_map/reduce_scatter | solution.py:188
  383.6 266.2 %reduce-scatter.20.cloned.1.call-start = ((), (), s32[]{:S(2)}) async-start(), calls=%async_computation.22 | async-start | bytes 2949120 | tf_op jit(solution)/shard_map/reduce_scatter | solution.py:188
  399.6 296.4 %reduce-scatter.10.cloned.1.call-start = ((), (), s32[]{:S(2)}) async-start(), calls=%async_computation.14 | async-start | bytes 3932160 | tf_op jit(solution)/shard_map/reduce_scatter | solution.py:188
  406.3 348.1 %all-reduce.9.cloned.1.call-start = ((), (), s32[]{:S(2)}) async-start(), calls=%async_computation.25 | async-start | bytes 2359296 | tf_op jit(solution)/shard_map/psum | solution.py:295
  696.0 4.0 copy-start.3
Sparse Core Ops, SparseCore 0:
  9.7 53.1 all-gather.12
  64.4 49.2 all-gather.16
  115.6 42.7 all-gather.22
  159.8 9.2 all-gather.10
  170.5 15.5 all-gather.14
  187.5 15.5 all-gather.18
  307.7 6.6 reduce-scatter.21
  317.3 9.8 reduce-scatter.11
  330.1 38.5 all-reduce.4
  370.9 12.5 reduce-scatter.13
  385.8 13.7 reduce-scatter.17
  405.7 110.5 all-reduce.6
  518.2 31.5 all-gather.20
  551.9 48.0 reduce-scatter.15
  602.1 47.5 reduce-scatter.19
  652.6 43.4 reduce-scatter.9
  699.0 55.2 all-reduce.8

commit v2 on v1

--- a/solution.py
+++ b/solution.py
@@ -180,12 +180,99 @@
     )(first, heads_in, heads_in, heads_in, grad_out, log_total)
 
 
+def partner(axis_name, step):
+    return lax.axis_index(axis_name) ^ step
+
+
+def swap(values, axis_name, step):
+    count = lax.axis_size(axis_name)
+    return lax.ppermute(values, axis_name, [(i, i ^ step) for i in range(count)])
+
+
+def direct(axis_name):
+    count = lax.axis_size(axis_name)
+    return count <= 4 and count & (count - 1) == 0
+
+
+def gather_into(values, axis_name, axis=0):
+    if not direct(axis_name):
+        return lax.all_gather(values, axis_name, axis=axis)
+    count = lax.axis_size(axis_name)
+    shape = values.shape[:axis] + (count,) + values.shape[axis:]
+    pieces = [swap(values, axis_name, step) for step in range(1, count)]
+    whole = jnp.zeros(shape, values.dtype)
+    for step, piece in enumerate([values] + pieces):
+        whole = lax.dynamic_update_index_in_dim(whole, piece, partner(axis_name, step), axis)
+    return whole
+
+
 def gather(values, axis_name, axis=0):
-    return lax.all_gather(values, axis_name, axis=axis, tiled=True)
-
-
-def scatter_sum(values, axis_name, axis=0):
-    return lax.psum_scatter(values, axis_name, scatter_dimension=axis, tiled=True)
+    whole = gather_into(values, axis_name, axis)
+    shape = list(values.shape)
+    shape[axis] *= lax.axis_size(axis_name)
+    return whole.reshape(shape)
+
+
+def exchange(values, axis_name, split, join):
+    if not direct(axis_name):
+        moved = jnp.moveaxis(values, split, 0)
+        moved = lax.all_to_all(moved, axis_name, split_axis=0, concat_axis=0, tiled=True)
+        return jnp.moveaxis(moved, 0, join)
+    pieces = []
+    for step in range(lax.axis_size(axis_name)):
+        piece = lax.dynamic_index_in_dim(values, partner(axis_name, step), split, keepdims=False)
+        pieces.append(swap(piece, axis_name, step) if step else piece)
+    shape = pieces[0].shape
+    whole = jnp.zeros(shape[:join] + (len(pieces),) + shape[join:], values.dtype)
+    for step, piece in enumerate(pieces):
+        whole = lax.dynamic_update_index_in_dim(whole, piece, partner(axis_name, step), join)
+    return whole
+
+
+def scatter_sum(values, axis_name, split=0):
+    if not direct(axis_name):
+        total = lax.psum_scatter(values, axis_name, scatter_dimension=split, tiled=False)
+        return total.astype(jnp.float32)
+    total = None
+    for step in reversed(range(lax.axis_size(axis_name))):
+        piece = lax.dynamic_index_in_dim(values, partner(axis_name, step), split, keepdims=False)
+        piece = (swap(piece, axis_name, step) if step else piece).astype(jnp.float32)
+        total = piece if total is None else total + piece
+    return total
+
+
+def small_sum(values, axis_names):
+    for axis_name in axis_names:
+        count = lax.axis_size(axis_name)
+        if count & (count - 1):
+            values = lax.psum(values, axis_name)
+            continue
+        step = 1
+        while step < count:
+            values = values + swap(values, axis_name, step)
+            step *= 2
+    return values
+
+
+def halves(values):
+    if lax.axis_size("shard") == 2:
+        return [values, swap(values, "shard", 1)]
+    return [lax.all_gather(values, "shard", axis=0, tiled=True)]
+
+
+def sum_halves(grads):
+    if len(grads) == 2:
+        received = swap(grads[1].astype(jnp.bfloat16), "shard", 1)
+        return (grads[0] + received.astype(jnp.float32)).astype(jnp.bfloat16)
+    return lax.psum_scatter(
+        grads[0].astype(jnp.bfloat16), "shard", scatter_dimension=0, tiled=True
+    )
+
+
+def shard_rows_sum(values):
+    shards = lax.axis_size("shard")
+    split = values.reshape((shards, values.shape[0] // shards) + values.shape[1:])
+    return scatter_sum(split, "shard").astype(jnp.bfloat16)
 
 
 def local(
@@ -208,10 +295,13 @@
     low, full = jnp.bfloat16, jnp.float32
     tok_count, width = tokens.shape[1], tokens.shape[2]
     parts = lax.axis_size("heads")
+    depth = lax.axis_size("tensor")
     mine = lax.axis_index("heads")
     part_width = width // parts
     head_count = part_width // HEAD_DIM
     shard_rows = w_qkv.shape[0]
+    hidden_rows = w_in.shape[0]
+    quarter = hidden_rows // parts
 
     group_tokens = gather(tokens[0], "heads")
     group_len = group_tokens.shape[0]
@@ -231,9 +321,12 @@
     ).astype(full)
     gain_one, shift_one, out_bias, gain_two, shift_two, back_bias = (vectors[i] for i in range(6))
     full_out = gather(w_out, "shard")
-    full_in = gather(gather(w_in, "tensor"), "shard")
-    full_back = gather(gather(w_back, "tensor"), "shard")
-    in_bias = gather(gather(bias_in, "tensor"), "shard").astype(full)
+
+    back_quarter = lax.dynamic_slice_in_dim(w_back, mine * quarter, quarter, 0)
+    back_quarter = lax.all_gather(back_quarter, "tensor", axis=0)
+    w_in, back_quarter = lax.optimization_barrier((w_in, back_quarter))
+    in_parts = halves(lax.all_gather(w_in, "tensor", axis=0, tiled=True))
+    bias_parts = halves(gather(bias_in, "tensor"))
 
     inputs = tokens[0].astype(full)
     _, norm_one_back = jax.vjp(layer_norm, inputs, gain_one, shift_one)
@@ -241,6 +334,8 @@
     own_bias = lax.dynamic_slice_in_dim(vectors[6:8], mine * part_width, part_width, 1)
     qkv_bias = jnp.concatenate([own_bias[0], jnp.zeros((part_width,), full), own_bias[1]])
     projected = (jnp.dot(attn_in, own_qkv, preferred_element_type=full) + qkv_bias).astype(low)
+    back_quarter, projected = lax.optimization_barrier((back_quarter, projected))
+    back_parts = halves(gather_into(back_quarter, "heads", 1).reshape(-1, width))
     shrink = jnp.where(jnp.arange(3 * part_width) < part_width, 1.0 / math.sqrt(HEAD_DIM), 1.0)
     heads_in = (
         (projected * shrink.astype(low))
@@ -251,39 +346,76 @@
         sequence_starts(seq_lengths[0], group_len)[:, None], (group_len, 128)
     )
     attended, log_total = attend(first, heads_in)
-    attended = attended.transpose(1, 0, 2).reshape(group_len, part_width)
-    back_tok = lax.all_to_all(attended, "heads", split_axis=0, concat_axis=1, tiled=True)
+    attended = attended.transpose(1, 0, 2).reshape(parts, tok_count, part_width)
+    back_tok = exchange(attended, "heads", 0, 1).reshape(tok_count, width)
     hidden_res = inputs + jnp.dot(back_tok, full_out, preferred_element_type=full) + out_bias
 
     normed_two, norm_two_back = jax.vjp(layer_norm, hidden_res, gain_two, shift_two)
     mlp_in = normed_two.astype(low)
     cot_rows = cotangent[0]
     cot_float = cot_rows.astype(full)
-    pre_act = contract_last(mlp_in, full_in) + in_bias
-    activated, gelu_back = jax.vjp(gelu_tanh, pre_act)
-    act_low = activated.astype(low)
-    branch = jnp.dot(act_low, full_back, preferred_element_type=full)
-    output = (hidden_res + branch + back_bias).astype(low)[None]
-    grad_w_back = contract_first(act_low, cot_rows).astype(low)
-    grad_act = contract_last(cot_rows, full_back)
-    grad_pre = gelu_back(grad_act)[0].astype(low)
-    grad_in_bias = jnp.sum(grad_pre.astype(full), axis=0)
-    grad_w_in = contract_first(grad_pre, mlp_in).astype(low)
-    grad_normed_two = jnp.dot(grad_pre, full_in, preferred_element_type=full)
+    result = hidden_res + back_bias
+    grad_normed_two = 0.0
+    grads_back, grads_in, grads_bias = [], [], []
+    for part_in, part_bias, part_back in zip(in_parts, bias_parts, back_parts):
+        pre_act = contract_last(mlp_in, part_in) + part_bias.astype(full)
+        activated, gelu_back = jax.vjp(gelu_tanh, pre_act)
+        act_low = activated.astype(low)
+        result = result + jnp.dot(act_low, part_back, preferred_element_type=full)
+        grads_back.append(contract_first(act_low, cot_rows))
+        grad_pre = gelu_back(contract_last(cot_rows, part_back))[0].astype(low)
+        grads_bias.append(jnp.sum(grad_pre.astype(full), axis=0))
+        grads_in.append(contract_first(grad_pre, mlp_in))
+        grad_normed_two += jnp.dot(grad_pre, part_in, preferred_element_type=full)
+    output = result.astype(low)[None]
     grad_res_norm, grad_gain_two, grad_shift_two = norm_two_back(grad_normed_two)
     grad_hidden = cot_float + grad_res_norm
     hidden_low = grad_hidden.astype(low)
     grad_w_out = contract_first(back_tok, hidden_low).astype(low)
 
     grad_attended = contract_last(hidden_low, full_out).astype(low)
-    grad_heads = lax.all_to_all(grad_attended, "heads", split_axis=1, concat_axis=0, tiled=True)
+    grad_heads = exchange(grad_attended.reshape(tok_count, parts, part_width), "heads", 1, 0)
+    sum_back, sum_in, sum_out = (
+        sum_halves(grads_back),
+        sum_halves(grads_in),
+        shard_rows_sum(grad_w_out),
+    )
+    grad_heads, sum_back, sum_in, sum_out = lax.optimization_barrier(
+        (grad_heads, sum_back, sum_in, sum_out)
+    )
+    by_part = (depth, parts, quarter, width)
+    part_back = scatter_sum(sum_back.reshape(by_part), "heads", 1)
+    part_in = scatter_sum(sum_in.reshape(by_part), "heads", 1)
+    part_out = scatter_sum(sum_out.reshape(parts, shard_rows // parts, width), "heads", 0)
     grad_heads = grad_heads.reshape(group_len, head_count, HEAD_DIM).transpose(1, 0, 2)
     grads = attend_back(first, heads_in, grad_heads, log_total)
+    grads, part_back, part_in, part_out = lax.optimization_barrier(
+        (grads, part_back.astype(low), part_in.astype(low), part_out.astype(low))
+    )
+    own_pair = lax.psum_scatter(
+        jnp.concatenate([part_back, part_in], axis=1),
+        "tensor",
+        scatter_dimension=0,
+        tiled=False,
+    )
+    part_out = lax.psum(part_out, "tensor")
     grad_proj = (
         jnp.concatenate(grads, axis=0).transpose(1, 0, 2).reshape(group_len, 3 * part_width)
     )
-    grad_attn_in = scatter_sum(contract_last(grad_proj, own_qkv).astype(low), "heads").astype(full)
-    grad_w_qkv = contract_first(attn_in, grad_proj).astype(low)
+    grad_w_qkv = shard_rows_sum(contract_first(attn_in, grad_proj).astype(low))
+    grad_attn_in = contract_last(grad_proj, own_qkv).astype(low)
+    grad_attn_in = scatter_sum(grad_attn_in.reshape(parts, tok_count, width), "heads")
+    grad_attn_in, own_pair, part_out = lax.optimization_barrier((grad_attn_in, own_pair, part_out))
+    own_three = gather_into(jnp.concatenate([own_pair, part_out], axis=0), "heads", 0)
+    own_back = own_three[:, :quarter].reshape(hidden_rows, width)
+    own_in = own_three[:, quarter : 2 * quarter].reshape(hidden_rows, width)
+    own_out = own_three[:, 2 * quarter :].reshape(shard_rows, width)
+
+    part_qkv = scatter_sum(
+        grad_w_qkv.reshape(depth, shard_rows // depth, 3 * part_width), "tensor"
+    ).astype(low)
+    part_qkv = gather(part_qkv, "tensor").reshape(shard_rows, 3, part_width)
+    own_grad_qkv = gather_into(part_qkv, "heads", 2).reshape(shard_rows, 3 * width)
     grad_proj_sum = jnp.sum(grad_proj.astype(full), axis=0).reshape(3, part_width)
     grad_qv_bias = lax.dynamic_update_slice_in_dim(
         jnp.zeros((2, width), full), grad_proj_sum[0::2], mine * part_width, 1
@@ -291,16 +423,14 @@
     grad_input_norm, grad_gain_one, grad_shift_one = norm_one_back(grad_attn_in)
     input_grad = (grad_hidden + grad_input_norm).astype(low)[None]
 
-    own_back = lax.psum(scatter_sum(scatter_sum(grad_w_back, "shard"), "tensor"), "heads")
-    own_in = lax.psum(scatter_sum(scatter_sum(grad_w_in, "shard"), "tensor"), "heads")
-    own_out = lax.psum(scatter_sum(grad_w_out, "shard"), ("heads", "tensor"))
-    part_qkv = lax.psum(scatter_sum(grad_w_qkv, "shard"), "tensor")
-    own_grad_qkv = (
-        lax.all_gather(part_qkv.reshape(shard_rows, 3, part_width), "heads", axis=2, tiled=True)
-        .reshape(shard_rows, 3 * width)
-        .astype(full)
-    )
-    sums = lax.psum(
+    shard = lax.axis_index("shard")
+    if len(grads_bias) == 2:
+        ordered = jnp.zeros((2, grads_bias[0].shape[0]), full)
+        ordered = lax.dynamic_update_index_in_dim(ordered, grads_bias[0], shard, 0)
+        grad_in_bias = lax.dynamic_update_index_in_dim(ordered, grads_bias[1], 1 - shard, 0)
+    else:
+        grad_in_bias = grads_bias[0]
+    sums = small_sum(
         jnp.concatenate(
             [
                 jnp.stack(
@@ -319,10 +449,8 @@
         ),
         ("shard", "heads", "tensor"),
     )
-    shard = lax.axis_index("shard")
     owned = lax.dynamic_slice_in_dim(sums[:8], shard * shard_rows, shard_rows, 1)
-    hidden_rows = bias_in.shape[0]
-    place = shard * lax.axis_size("tensor") + lax.axis_index("tensor")
+    place = shard * depth + lax.axis_index("tensor")
     own_in_bias = lax.dynamic_slice_in_dim(
         sums[8:].reshape(-1), place * hidden_rows, hidden_rows, 0
     )
@@ -331,7 +459,7 @@
         input_grad,
         owned[0],
         owned[1],
-        own_grad_qkv,
+        own_grad_qkv.astype(full),
         owned[6:8],
         own_out.astype(full),
         owned[2],

time: 775 us -> 494 us (0.64)
  waiting for transfers between devices: 492 us -> 70.7 us
  local copies, waits for them, and re-layouts: 42.8 us -> 180 us
  starting transfers between devices: 4.46 us -> 69.4 us
  blocking collectives: 74.3 us -> 15.9 us
  matrix products: 66.1 us -> 55.8 us
    all_gather x7 -> x1, waiting for transfers between devices: 172 us -> 0.01 us  [local(): in_parts = halves(lax.all_gather(w_in, 'tensor', axis=0, tiled=True))]
    reduce_scatter x6 -> x1, waiting for transfers between devices: 168 us -> 0.01 us  [local(): lax.psum_scatter(jnp.concatenate([part_back, part_in], axis=1), 'tensor',...]
    psum x3 -> x1, waiting for transfers between devices: 145 us -> 0.01 us  [local(): part_out = lax.psum(part_out, 'tensor')]
    dynamic_update_slice x0 -> x40, local copies, waits for them, and re-layouts: none -> 105 us  [the longest x30 81.8 us: gather_into(): lax.dynamic_update_index_in_dim(whole, piece, partner(axis_name, step), a...]
    ppermute x0 -> x54, waiting for transfers between devices: none -> 70.6 us  [swap(): lax.ppermute(values, axis_name, [(i, i ^ step) for i in range(count)])]
    ppermute x0 -> x54, starting transfers between devices: none -> 69.3 us  [swap(): lax.ppermute(values, axis_name, [(i, i ^ step) for i in range(count)])]
    psum x1 -> x0, blocking collectives: 39.9 us -> none  [local(): lax.psum(jnp.concatenate([jnp.stack([grad_gain_one, grad_shift_one, jnp.s...]
    broadcast_in_dim x0 -> x29, local copies, waits for them, and re-layouts: none -> 16.5 us  [the longest x11 7.09 us: gather_into(): lax.dynamic_update_index_in_dim(whole, piece, partner(axis_name, step), a...]
  transfers between devices with their start and end apart: 18 -> 57, of which waited for: 13 -> 14; matrix products, arithmetic and copies ran while one was open for 11% -> 48% of each run, Pallas kernels for 2% -> 9%
where the time goes in v2:
time: 494 us; the launch traced here: 485 us
  local copies, waits for them, and re-layouts  180 us (36%)
  waiting for transfers between devices  70.7 us (14%)
  starting transfers between devices  69.4 us (14%)
  matrix products  55.8 us (11%)
  Pallas kernels  45.9 us (9%)
  other arithmetic  32.5 us (7%)
  blocking collectives  15.9 us (3%)
  between operations  15.1 us (3%)
    dynamic_update_slice x30, local copies, waits for them, and re-layouts, gather_into(): lax.dynamic_update_index_in_dim(whole, piece, partner(axis_name, step), a...  81.8 us
    ppermute x54, waiting for transfers between devices, swap(): lax.ppermute(values, axis_name, [(i, i ^ step) for i in range(count)])  70.6 us
    ppermute x54, starting transfers between devices, swap(): lax.ppermute(values, axis_name, [(i, i ^ step) for i in range(count)])  69.3 us
    pallas_call x1, Pallas kernels, attend_back(): pl.pallas_call(attend_back_kernel, grid=(head_count,), in_specs=[pl.Block...  28 us
    dynamic_update_slice x8, local copies, waits for them, and re-layouts, exchange(): lax.dynamic_update_index_in_dim(whole, piece, partner(axis_name, step), j...  22.6 us
    dot_general x6, matrix products, contract_first(): lax.dot_general(left, right, (((0,), (0,)), ((), ())), preferred_element_...  21.7 us
    unnamed x110, local copies, waits for them, and re-layouts  18.1 us
    pallas_call x1, Pallas kernels, attend(): pl.pallas_call(attend_kernel, grid=(head_count,), in_specs=[pl.BlockSpec(...  17.9 us
  transfers between devices with their start and end apart: 57, of which 14 were waited for; matrix products, arithmetic and copies ran while one was open for 48% of the time, Pallas kernels for 9%

profile of v2, /device:TPU:0, one launch (start us, length us, event | category | flops | bytes accessed | tf_op | source)
XLA Modules:
  0.0 484.8 jit_solution(2755397842526126924)
XLA Ops:
  7.2 3.0 collective-permute-start
  13.3 2.6 collective-permute-start.10
  16.2 15.9 %all-gather = bf16[384,768]{1,0:T(8,128)(2,1)} all-gather(bf16[96,768]{1,0:T(8,128)(2,1)S(1)} %constant_dynamic-slice_fusion.9), channel_id=2, replica_groups=mesh['shard'=2,'heads'=4,'tensor'=4] {'tensor'}, dimensions={0}, use_global_device_ids=true | all-gather | bytes 737280 | tf_op jit(solution)/shard_map/all_gather | solution.py:326
  36.9 3.9 copy.88
  48.4 2.6 copy.89
  52.3 16.5 %dynamic_update_slice.141 = bf16[2,384,576]{1,0,2:T(2,128)(2,1)} dynamic-update-slice(bf16[2,384,576]{1,0,2:T(2,128)(2,1)} %broadcast_in_dim.237, bf16[1,384,576]{1,0,2:T(2,128)(2,1)} %copy.89, s32[]{:T(128)S(6)} %select_n.146, s32[]{:T(128)} %constant.249.clone.1, s32[]{:T(128)} %constant.249.clone.1) | dynamic-update-slice | bytes 884740 | tf_op jit(solution)/shard_map/jit(dynamic_update_index_in_dim)/dynamic_update_slice | solution.py:205
  71.6 2.6 copy.90
  74.2 16.3 %dynamic_update_slice.142 = bf16[2,384,576]{1,0,2:T(2,128)(2,1)} dynamic-update-slice(bf16[2,384,576]{1,0,2:T(2,128)(2,1)} %dynamic_update_slice.141, bf16[1,384,576]{1,0,2:T(2,128)(2,1)} %copy.90, s32[]{:T(128)S(6)} %select_n.147, s32[]{:T(128)} %constant.249.clone.1, s32[]{:T(128)} %constant.249.clone.1) | dynamic-update-slice | bytes 884740 | tf_op jit(solution)/shard_map/jit(dynamic_update_index_in_dim)/dynamic_update_slice | solution.py:205
  91.9 2.2 bitcast_dynamic-update-slice_fusion.7
  100.7 2.0 add_convert_fusion.2
  106.5 4.0 copy.91
  110.8 17.9 %shard_map.254 = (bf16[3,2048,64]{2,1,0:T(8,128)(2,1)S(1)}, f32[3,2048,128]{2,1,0:T(8,128)S(1)}) custom-call(s32[2048,128]{1,0:T(8,128)S(1)} %broadcast_in_dim.229.first_ref, bf16[9,2048,64]{2,1,0:T(8,128)(2,1)} %bitcast.267, bf16[9,2048,64]{2,1,0:T(8,128)(2,1)} %bitcast.268, bf16[9,2048,64]{2,1,0:T(8,128)(2,1)} %bitcast.269), custom_call_target="tpu_custom_call" | custom-call | flops 2013265920 | bytes 9437184 | tf_op jit(solution)/shard_map/pallas_call | solution.py:143
  140.0 2.4 collective-permute-start.7
  142.5 4.2 collective-permute-done.7
  146.6 2.5 fusion.55
  150.7 2.1 bitcast_dynamic-update-slice_fusion.4
  158.5 3.3 convert_reduce_fusion.3
  164.7 3.2 convolution_convert_fusion.1
  167.9 4.0 convert_reduce_fusion.2
  171.9 2.9 convolution_convert_fusion
  174.7 2.3 multiply_reduce_fusion
  182.0 3.0 convolution_convert_fusion.5
  190.1 4.1 collective-permute-done.18
  194.2 2.4 collective-permute-start.20
  197.1 3.3 dynamic_update_slice.157
  202.6 2.1 copy.100
  204.6 6.4 %dynamic_update_slice.158 = bf16[4,512,192]{1,0,2:T(4,128)(2,1)S(1)} dynamic-update-slice(bf16[4,512,192]{1,0,2:T(4,128)(2,1)S(1)} %dynamic_update_slice.157, bf16[1,512,192]{1,0,2:T(2,128)(2,1)} %copy.98, s32[]{:T(128)S(6)} %select_n.143, s32[]{:T(128)} %constant.249.clone.1, s32[]{:T(128)} %constant.249.clone.1) | dynamic-update-slice | bytes 393220 | tf_op jit(solution)/shard_map/jit(dynamic_update_index_in_dim)/dynamic_update_slice | solution.py:228
  211.0 6.4 %dynamic_update_slice.159 = bf16[4,512,192]{1,0,2:T(4,128)(2,1)S(1)} dynamic-update-slice(bf16[4,512,192]{1,0,2:T(4,128)(2,1)S(1)} %dynamic_update_slice.158, bf16[1,512,192]{1,0,2:T(2,128)(2,1)} %copy.99, s32[]{:T(128)S(6)} %select_n.144, s32[]{:T(128)} %constant.249.clone.1, s32[]{:T(128)} %constant.249.clone.1) | dynamic-update-slice | bytes 393220 | tf_op jit(solution)/shard_map/jit(dynamic_update_index_in_dim)/dynamic_update_slice | solution.py:228
  217.4 6.4 %dynamic_update_slice.160 = bf16[4,512,192]{1,0,2:T(4,128)(2,1)S(1)} dynamic-update-slice(bf16[4,512,192]{1,0,2:T(4,128)(2,1)S(1)} %dynamic_update_slice.159, bf16[1,512,192]{1,0,2:T(2,128)(2,1)} %copy.100, s32[]{:T(128)S(6)} %select_n.145, s32[]{:T(128)} %constant.249.clone.1, s32[]{:T(128)} %constant.249.clone.1) | dynamic-update-slice | bytes 393220 | tf_op jit(solution)/shard_map/jit(dynamic_update_index_in_dim)/dynamic_update_slice | solution.py:228
  223.9 2.2 fusion.31
  226.1 4.7 add_convert_fusion.1
  230.9 5.4 %add_convert_fusion = bf16[1536,768]{1,0:T(8,128)(2,1)} fusion(bf16[1536,768]{1,0:T(8,128)(2,1)} %collective-permute-done.22, bf16[512,1536]{1,0:T(8,128)(2,1)S(1)} %copy-done.47, bf16[512,768]{1,0:T(8,128)(2,1)S(1)} %copy-done.30), kind=kOutput, calls=%fused_computation.10 | convolution fusion | flops 1211498496 | bytes 7077888 | tf_op jit(solution)/shard_map/dot_general | solution.py:38
  246.1 2.7 dynamic-slice_bitcast_fusion.5
  248.8 8.4 %collective-permute-done.32 = bf16[96,768]{1,0:T(8,128)(2,1)S(1)} collective-permute-done((bf16[96,768]{1,0:T(8,128)(2,1)S(1)}, bf16[96,768]{1,0:T(8,128)(2,1)S(1)}, u32[]{:S(2)}, u32[]{:S(2)}) %collective-permute-start.32) | collective-permute-done | bytes 147488 | tf_op jit(solution)/shard_map/ppermute | solution.py:189
  257.7 16.5 %collective-permute-done.31 = bf16[96,768]{1,0:T(8,128)(2,1)S(1)} collective-permute-done((bf16[96,768]{1,0:T(8,128)(2,1)S(1)}, bf16[96,768]{1,0:T(8,128)(2,1)S(1)}, u32[]{:S(2)}, u32[]{:S(2)}) %collective-permute-start.31) | collective-permute-done | bytes 147488 | tf_op jit(solution)/shard_map/ppermute | solution.py:189
  277.7 28.0 %shard_map.255 = (bf16[3,2048,64]{2,1,0:T(8,128)(2,1)S(1)}, bf16[3,2048,64]{2,1,0:T(8,128)(2,1)S(1)}, bf16[3,2048,64]{2,1,0:T(8,128)(2,1)S(1)}) custom-call(s32[2048,128]{1,0:T(8,128)S(1)} %broadcast_in_dim.229.first_ref, bf16[9,2048,64]{2,1,0:T(8,128)(2,1)} %bitcast.270, bf16[9,2048,64]{2,1,0:T(8,128)(2,1)} %bitcast.271, bf16[9,2048,64]{2,1,0:T(8,128)(2,1)} %bitcast.272, ...), custom_call_target="tpu_custom_call" | custom-call | flops 5033164800 | bytes 12582912 | tf_op jit(solution)/shard_map/pallas_call | solution.py:165
  309.7 2.9 fusion.30
  312.5 2.7 fusion.29
  315.2 3.7 convert_reduce_fusion
  318.9 4.6 copy.103
  325.1 4.8 convolution_convert_fusion.4
  329.9 2.3 reshape.338
  334.9 5.2 %fusion.50 = f32[512,768]{1,0:T(8,128)} fusion(bf16[1536,768]{1,0:T(8,128)(2,1)S(1)} %bitcast.289, f32[512,1536]{1,0:T(8,128)} %copy-done.45, f32[1536]{0:T(1024)S(1)} %convert_element_type.254), kind=kOutput, calls=%fused_computation.187 | convolution fusion | flops 1215823872 | bytes 7084032 | tf_op jit(solution)/shard_map/dot_general | solution.py:364
  342.8 2.4 collective-permute-start.44
  345.2 2.5 collective-permute-start.43
  347.7 4.7 convolution_convert_fusion.2
  352.4 7.2 %collective-permute-done.43 = bf16[96,576]{1,0:T(8,128)(2,1)S(1)} collective-permute-done((bf16[96,576]{1,0:T(8,128)(2,1)S(1)}, bf16[96,576]{1,0:T(8,128)(2,1)S(1)}, u32[]{:S(2)}, u32[]{:S(2)}) %collective-permute-start.43) | collective-permute-done | bytes 110624 | tf_op jit(solution)/shard_map/ppermute | solution.py:189
  359.7 2.8 collective-permute-start.45
  368.0 2.0 collective-permute-start.47
  370.0 2.9 fusion.34
  375.6 6.6 %dynamic_update_slice.164 = bf16[4,96,576]{1,0,2:T(4,128)(2,1)S(1)} dynamic-update-slice(bf16[4,96,576]{1,0,2:T(4,128)(2,1)S(1)} %broadcast_in_dim.276, bf16[1,96,576]{1,0,2:T(2,128)(2,1)S(1)} %copy.107, s32[]{:T(128)S(6)} %select_n.150, s32[]{:T(128)} %constant.249.clone.1, s32[]{:T(128)} %constant.249.clone.1) | dynamic-update-slice | bytes 221188 | tf_op jit(solution)/shard_map/jit(dynamic_update_index_in_dim)/dynamic_update_slice | solution.py:205
  384.2 6.6 %dynamic_update_slice.165 = bf16[4,96,576]{1,0,2:T(4,128)(2,1)S(1)} dynamic-update-slice(bf16[4,96,576]{1,0,2:T(4,128)(2,1)S(1)} %dynamic_update_slice.164, bf16[1,96,576]{1,0,2:T(2,128)(2,1)S(1)} %copy.108, s32[]{:T(128)S(6)} %select_n.151, s32[]{:T(128)} %constant.249.clone.1, s32[]{:T(128)} %constant.249.clone.1) | dynamic-update-slice | bytes 221188 | tf_op jit(solution)/shard_map/jit(dynamic_update_index_in_dim)/dynamic_update_slice | solution.py:205
  390.8 6.6 %dynamic_update_slice.166 = bf16[4,96,576]{1,0,2:T(4,128)(2,1)S(1)} dynamic-update-slice(bf16[4,96,576]{1,0,2:T(4,128)(2,1)S(1)} %dynamic_update_slice.165, bf16[1,96,576]{1,0,2:T(2,128)(2,1)S(1)} %copy.109, s32[]{:T(128)S(6)} %select_n.152, s32[]{:T(128)} %constant.249.clone.1, s32[]{:T(128)} %constant.249.clone.1) | dynamic-update-slice | bytes 221188 | tf_op jit(solution)/shard_map/jit(dynamic_update_index_in_dim)/dynamic_update_slice | solution.py:205
  397.4 6.6 %dynamic_update_slice.167 = bf16[4,96,576]{1,0,2:T(4,128)(2,1)S(1)} dynamic-update-slice(bf16[4,96,576]{1,0,2:T(4,128)(2,1)S(1)} %dynamic_update_slice.166, bf16[1,96,576]{1,0,2:T(2,128)(2,1)S(1)} %copy.110, s32[]{:T(128)S(6)} %select_n.153, s32[]{:T(128)} %constant.249.clone.1, s32[]{:T(128)} %constant.249.clone.1) | dynamic-update-slice | bytes 221188 | tf_op jit(solution)/shard_map/jit(dynamic_update_index_in_dim)/dynamic_update_slice | solution.py:205
  411.3 2.0 convert_add_fusion.2
  413.3 5.5 %collective-permute-done.48 = bf16[384,3,192]{0,2,1:T(8,128)(2,1)S(1)} collective-permute-done((bf16[384,3,192]{0,2,1:T(8,128)(2,1)}, bf16[384,3,192]{0,2,1:T(8,128)(2,1)S(1)}, u32[]{:S(2)}, u32[]{:S(2)}) %collective-permute-start.48) | collective-permute-done | bytes 442400 | tf_op jit(solution)/shard_map/ppermute | solution.py:189
  419.6 5.5 %collective-permute-done.49 = bf16[384,3,192]{0,2,1:T(8,128)(2,1)S(1)} collective-permute-done((bf16[384,3,192]{0,2,1:T(8,128)(2,1)}, bf16[384,3,192]{0,2,1:T(8,128)(2,1)S(1)}, u32[]{:S(2)}, u32[]{:S(2)}) %collective-permute-start.49) | collective-permute-done | bytes 442400 | tf_op jit(solution)/shard_map/ppermute | solution.py:189
  433.5 2.0 collective-permute-done.37
  436.7 2.9 collective-permute-done.38
  440.2 10.1 %collective-permute-start.39 = (f32[12,768]{1,0:T(8,128)}, f32[12,768]{1,0:T(8,128)}, u32[]{:S(2)}, u32[]{:S(2)}) collective-permute-start(f32[12,768]{1,0:T(8,128)} %add.399), channel_id=1, source_target_pairs={{0,1},{1,0},{2,3},{3,2},{4,5},{5,4},{6,7},{7,6},{8,9},{9,8},{10,11... | collective-permute-start | bytes 110600 | tf_op jit(solution)/shard_map/ppermute | solution.py:189
  452.1 2.9 copy.114
  455.0 2.0 collective-permute-start.53
  457.8 3.3 collective-permute-start.40
  466.3 8.8 %collective-permute-done.52 = bf16[288,768]{1,0:T(8,128)(2,1)S(1)} collective-permute-done((bf16[288,768]{1,0:T(8,128)(2,1)}, bf16[288,768]{1,0:T(8,128)(2,1)S(1)}, u32[]{:S(2)}, u32[]{:S(2)}) %collective-permute-start.52) | collective-permute-done | bytes 442400 | tf_op jit(solution)/shard_map/ppermute | solution.py:189
  (358 shorter events, 129.5 us)
Async XLA Ops:
  7.2 143.5 %all-gather.3.cloned.1.call-start = ((), (), s32[]{:S(2)}) async-start(), calls=%async_computation.1 | async-start | bytes 2949120 | tf_op jit(solution)/shard_map/all_gather | solution.py:328
  7.2 86.9 %collective-permute-start = (bf16[512,768]{1,0:T(8,128)(2,1)}, bf16[512,768]{1,0:T(8,128)(2,1)}, u32[]{:S(2)}, u32[]{:S(2)}) collective-permute-start(bf16[512,768]{1,0:T(8,128)(2,1)} %bitcast.273), channel_id=1, source_target_pairs={{0,4},{4,0},{8,12},{12,8},{1,5},{5,1},{9,13},{13,9},{2,6},{6,2},{1... | collective-permute-start | bytes 2359304 | tf_op jit(solution)/shard_map/ppermute | solution.py:189
  10.2 85.1 %collective-permute-start.1 = (bf16[512,768]{1,0:T(8,128)(2,1)}, bf16[512,768]{1,0:T(8,128)(2,1)}, u32[]{:S(2)}, u32[]{:S(2)}) collective-permute-start(bf16[512,768]{1,0:T(8,128)(2,1)} %bitcast.274), channel_id=1, source_target_pairs={{0,8},{4,12},{8,0},{12,4},{1,9},{5,13},{9,1},{13,5},{2,10},{6,14},... | collective-permute-start | bytes 2359304 | tf_op jit(solution)/shard_map/ppermute | solution.py:189
  11.8 35.7 %collective-permute-start.9 = (bf16[384]{0:T(512)(128)(2,1)}, bf16[384]{0:T(512)(128)(2,1)S(1)}, u32[]{:S(2)}, u32[]{:S(2)}) collective-permute-start(bf16[384]{0:T(512)(128)(2,1)} %param.25), channel_id=1, source_target_pairs={{0,1},{1,0},{2,3},{3,2},{4,5},{5,4},{6,7},{7,6},{8,9},{9,8},{10,11... | collective-permute-start | bytes 2312 | tf_op jit(solution)/shard_map/ppermute | solution.py:189
  13.3 34.3 %collective-permute-start.10 = (bf16[384]{0:T(512)(128)(2,1)}, bf16[384]{0:T(512)(128)(2,1)S(1)}, u32[]{:S(2)}, u32[]{:S(2)}) collective-permute-start(bf16[384]{0:T(512)(128)(2,1)} %param.25), channel_id=1, source_target_pairs={{0,2},{1,3},{2,0},{3,1},{4,6},{5,7},{6,4},{7,5},{8,10},{9,11},{10,... | collective-permute-start | bytes 2312 | tf_op jit(solution)/shard_map/ppermute | solution.py:189
  15.9 32.3 %collective-permute-start.11 = (bf16[384]{0:T(512)(128)(2,1)}, bf16[384]{0:T(512)(128)(2,1)S(1)}, u32[]{:S(2)}, u32[]{:S(2)}) collective-permute-start(bf16[384]{0:T(512)(128)(2,1)} %param.25), channel_id=1, source_target_pairs={{0,3},{1,2},{2,1},{3,0},{4,7},{5,6},{6,5},{7,4},{8,11},{9,10},{10,... | collective-permute-start | bytes 2312 | tf_op jit(solution)/shard_map/ppermute | solution.py:189
  16.2 24.6 %copy-start.44 = (s32[1,4]{1,0:T(1,128)S(1)}, s32[1,4]{1,0:T(1,128)}, u32[]{:S(2)}) copy-start(s32[1,4]{1,0:T(1,128)} %param.28) | copy-start | bytes 52
  32.1 393.9 %all-reduce.2.cloned.1.call-start = ((), (), s32[]{:S(2)}) async-start(), calls=%async_computation.3 | async-start | bytes 294912 | tf_op jit(solution)/shard_map/psum | solution.py:401
  47.5 22.0 %collective-permute-start.3 = (bf16[8,384]{1,0:T(8,128)(2,1)S(1)}, bf16[8,384]{1,0:T(8,128)(2,1)S(1)}, u32[]{:S(2)}, u32[]{:S(2)}) collective-permute-start(bf16[8,384]{1,0:T(8,128)(2,1)S(1)} %concatenate.18), channel_id=1, source_target_pairs={{0,16},{16,0},{1,17},{17,1},{2,18},{18,2},{3,19},{19,3},{4,20},{20... | collective-permute-start | bytes 18440 | tf_op jit(solution)/shard_map/ppermute | solution.py:189
  47.6 44.3 %collective-permute-start.8 = (bf16[384,768]{1,0:T(8,128)(2,1)}, bf16[384,768]{1,0:T(8,128)(2,1)}, u32[]{:S(2)}, u32[]{:S(2)}) collective-permute-start(bf16[384,768]{1,0:T(8,128)(2,1)} %param.20), channel_id=1, source_target_pairs={{0,16},{16,0},{1,17},{17,1},{2,18},{18,2},{3,19},{19,3},{4,20},{20... | collective-permute-start | bytes 1769480 | tf_op jit(solution)/shard_map/ppermute | solution.py:189
  48.3 20.6 %collective-permute-start.16 = (bf16[1536]{0:T(1024)(128)(2,1)S(1)}, bf16[1536]{0:T(1024)(128)(2,1)S(1)}, u32[]{:S(2)}, u32[]{:S(2)}) collective-permute-start(bf16[1536]{0:T(1024)(128)(2,1)S(1)} %reshape.322), channel_id=1, source_target_pairs={{0,16},{16,0},{1,17},{17,1},{2,18},{18,2},{3,19},{19,3},{4,20},{20... | collective-permute-start | bytes 9224 | tf_op jit(solution)/shard_map/ppermute | solution.py:189
  68.9 27.7 %collective-permute-start.2 = (bf16[512,768]{1,0:T(8,128)(2,1)}, bf16[512,768]{1,0:T(8,128)(2,1)}, u32[]{:S(2)}, u32[]{:S(2)}) collective-permute-start(bf16[512,768]{1,0:T(8,128)(2,1)} %bitcast.275), channel_id=1, source_target_pairs={{0,12},{4,8},{8,4},{12,0},{1,13},{5,9},{9,5},{13,1},{2,14},{6,10},... | collective-permute-start | bytes 2359304 | tf_op jit(solution)/shard_map/ppermute | solution.py:189
  69.5 2.1 collective-permute-start.4
  102.7 48.0 %collective-permute-start.12 = (bf16[4,96,768]{2,1,0:T(8,128)(2,1)}, bf16[4,96,768]{2,1,0:T(8,128)(2,1)}, u32[]{:S(2)}, u32[]{:S(2)}) collective-permute-start(bf16[4,96,768]{2,1,0:T(8,128)(2,1)} %bitcast.3), channel_id=1, source_target_pairs={{0,4},{4,0},{8,12},{12,8},{1,5},{5,1},{9,13},{13,9},{2,6},{6,2},{1... | collective-permute-start | bytes 1769480 | tf_op jit(solution)/shard_map/ppermute | solution.py:189
  104.2 48.6 %collective-permute-start.13 = (bf16[4,96,768]{2,1,0:T(8,128)(2,1)}, bf16[4,96,768]{2,1,0:T(8,128)(2,1)}, u32[]{:S(2)}, u32[]{:S(2)}) collective-permute-start(bf16[4,96,768]{2,1,0:T(8,128)(2,1)} %bitcast.3), channel_id=1, source_target_pairs={{0,8},{4,12},{8,0},{12,4},{1,9},{5,13},{9,1},{13,5},{2,10},{6,14},... | collective-permute-start | bytes 1769480 | tf_op jit(solution)/shard_map/ppermute | solution.py:189
  105.7 49.0 %collective-permute-start.14 = (bf16[4,96,768]{2,1,0:T(8,128)(2,1)}, bf16[4,96,768]{2,1,0:T(8,128)(2,1)}, u32[]{:S(2)}, u32[]{:S(2)}) collective-permute-start(bf16[4,96,768]{2,1,0:T(8,128)(2,1)} %bitcast.3), channel_id=1, source_target_pairs={{0,12},{4,8},{8,4},{12,0},{1,13},{5,9},{9,5},{13,1},{2,14},{6,10},... | collective-permute-start | bytes 1769480 | tf_op jit(solution)/shard_map/ppermute | solution.py:189
  133.8 6.2 %collective-permute-start.5 = (bf16[512,192]{0,1:T(8,128)(2,1)S(1)}, bf16[512,192]{0,1:T(8,128)(2,1)S(1)}, u32[]{:S(2)}, u32[]{:S(2)}) collective-permute-start(bf16[512,192]{0,1:T(8,128)(2,1)S(1)} %bitcast.312), channel_id=1, source_target_pairs={{0,4},{4,0},{8,12},{12,8},{1,5},{5,1},{9,13},{13,9},{2,6},{6,2},{1... | collective-permute-start | bytes 589832 | tf_op jit(solution)/shard_map/ppermute | solution.py:189
  135.3 7.1 %collective-permute-start.6 = (bf16[512,192]{0,1:T(8,128)(2,1)S(1)}, bf16[512,192]{0,1:T(8,128)(2,1)S(1)}, u32[]{:S(2)}, u32[]{:S(2)}) collective-permute-start(bf16[512,192]{0,1:T(8,128)(2,1)S(1)} %bitcast.311), channel_id=1, source_target_pairs={{0,8},{4,12},{8,0},{12,4},{1,9},{5,13},{9,1},{13,5},{2,10},{6,14},... | collective-permute-start | bytes 589832 | tf_op jit(solution)/shard_map/ppermute | solution.py:189
  138.4 10.8 %copy-start.18 = (bf16[4,4,96,768]{3,2,1,0:T(8,128)(2,1)}, bf16[4,4,96,768]{3,2,1,0:T(8,128)(2,1)S(1)}, u32[]{:S(2)}) copy-start(bf16[4,4,96,768]{3,2,1,0:T(8,128)(2,1)S(1)} %bitcast_dynamic-update-slice_fusion.5) | copy-start | bytes 7077892
  140.0 6.6 %collective-permute-start.7 = (bf16[512,192]{0,1:T(8,128)(2,1)S(1)}, bf16[512,192]{0,1:T(8,128)(2,1)S(1)}, u32[]{:S(2)}, u32[]{:S(2)}) collective-permute-start(bf16[512,192]{0,1:T(8,128)(2,1)S(1)} %bitcast.310), channel_id=1, source_target_pairs={{0,12},{4,8},{8,4},{12,0},{1,13},{5,9},{9,5},{13,1},{2,14},{6,10},... | collective-permute-start | bytes 589832 | tf_op jit(solution)/shard_map/ppermute | solution.py:189
  149.1 28.4 %copy-start.8 = (f32[512,768]{1,0:T(8,128)}, f32[512,768]{1,0:T(8,128)S(1)}, u32[]{:S(2)}) copy-start(f32[512,768]{1,0:T(8,128)S(1)} %get-tuple-element.161) | copy-start | bytes 4718596
  150.7 12.6 %collective-permute-start.15 = (bf16[1536,768]{1,0:T(8,128)(2,1)}, bf16[1536,768]{1,0:T(8,128)(2,1)S(1)}, u32[]{:S(2)}, u32[]{:S(2)}) collective-permute-start(bf16[1536,768]{1,0:T(8,128)(2,1)} %all-gather.3.cloned.1.call-done), channel_id=1, source_target_pairs={{0,16},{16,0},{1,17},{17,1},{2,18},{18,2},{3,19},{19,3},{4,20},{20... | collective-permute-start | bytes 7077896 | tf_op jit(solution)/shard_map/ppermute | solution.py:189
  156.6 11.3 %collective-permute-start.17 = (bf16[1536,768]{1,0:T(8,128)(2,1)}, bf16[1536,768]{1,0:T(8,128)(2,1)S(1)}, u32[]{:S(2)}, u32[]{:S(2)}) collective-permute-start(bf16[1536,768]{1,0:T(8,128)(2,1)} %bitcast.287), channel_id=1, source_target_pairs={{0,16},{16,0},{1,17},{17,1},{2,18},{18,2},{3,19},{19,3},{4,20},{20... | collective-permute-start | bytes 7077896 | tf_op jit(solution)/shard_map/ppermute | solution.py:189
  177.0 49.1 %collective-permute-start.21 = (bf16[1536,768]{1,0:T(8,128)(2,1)}, bf16[1536,768]{1,0:T(8,128)(2,1)}, u32[]{:S(2)}, u32[]{:S(2)}) collective-permute-start(bf16[1536,768]{1,0:T(8,128)(2,1)} %convolution_convert_fusion.1), channel_id=1, source_target_pairs={{0,16},{16,0},{1,17},{17,1},{2,18},{18,2},{3,19},{19,3},{4,20},{20... | collective-permute-start | bytes 7077896 | tf_op jit(solution)/shard_map/ppermute | solution.py:189
  177.4 53.5 %collective-permute-start.22 = (bf16[1536,768]{1,0:T(8,128)(2,1)}, bf16[1536,768]{1,0:T(8,128)(2,1)}, u32[]{:S(2)}, u32[]{:S(2)}) collective-permute-start(bf16[1536,768]{1,0:T(8,128)(2,1)} %convolution_convert_fusion), channel_id=1, source_target_pairs={{0,16},{16,0},{1,17},{17,1},{2,18},{18,2},{3,19},{19,3},{4,20},{20... | collective-permute-start | bytes 7077896 | tf_op jit(solution)/shard_map/ppermute | solution.py:189
  181.7 42.2 %collective-permute-start.23 = (bf16[384,768]{1,0:T(8,128)(2,1)}, bf16[384,768]{1,0:T(8,128)(2,1)}, u32[]{:S(2)}, u32[]{:S(2)}) collective-permute-start(bf16[384,768]{1,0:T(8,128)(2,1)} %dynamic-slice_bitcast_fusion.9), channel_id=1, source_target_pairs={{0,16},{16,0},{1,17},{17,1},{2,18},{18,2},{3,19},{19,3},{4,20},{20... | collective-permute-start | bytes 1769480 | tf_op jit(solution)/shard_map/ppermute | solution.py:189
  187.2 7.0 %collective-permute-start.18 = (bf16[512,192]{0,1:T(8,128)(2,1)S(1)}, bf16[512,192]{0,1:T(8,128)(2,1)S(1)}, u32[]{:S(2)}, u32[]{:S(2)}) collective-permute-start(bf16[512,192]{0,1:T(8,128)(2,1)S(1)} %get-tuple-element.144), channel_id=1, source_target_pairs={{0,4},{4,0},{8,12},{12,8},{1,5},{5,1},{9,13},{13,9},{2,6},{6,2},{1... | collective-permute-start | bytes 589832 | tf_op jit(solution)/shard_map/ppermute | solution.py:189
  188.6 12.9 %collective-permute-start.19 = (bf16[512,192]{0,1:T(8,128)(2,1)}, bf16[512,192]{0,1:T(8,128)(2,1)S(1)}, u32[]{:S(2)}, u32[]{:S(2)}) collective-permute-start(bf16[512,192]{0,1:T(8,128)(2,1)} %get-tuple-element.143), channel_id=1, source_target_pairs={{0,8},{4,12},{8,0},{12,4},{1,9},{5,13},{9,1},{13,5},{2,10},{6,14},... | collective-permute-start | bytes 589832 | tf_op jit(solution)/shard_map/ppermute | solution.py:189
  194.2 8.3 %collective-permute-start.20 = (bf16[512,192]{0,1:T(8,128)(2,1)}, bf16[512,192]{0,1:T(8,128)(2,1)}, u32[]{:S(2)}, u32[]{:S(2)}) collective-permute-start(bf16[512,192]{0,1:T(8,128)(2,1)} %get-tuple-element.142), channel_id=1, source_target_pairs={{0,12},{4,8},{8,4},{12,0},{1,13},{5,9},{9,5},{13,1},{2,14},{6,10},... | collective-permute-start | bytes 589832 | tf_op jit(solution)/shard_map/ppermute | solution.py:189
  202.5 23.6 %copy-start.14 = (bf16[1,512,768]{2,1,0:T(8,128)(2,1)S(1)}, bf16[1,512,768]{2,1,0:T(8,128)(2,1)}, u32[]{:S(2)}) copy-start(bf16[1,512,768]{2,1,0:T(8,128)(2,1)} %param.29) | copy-start | bytes 2359300
  237.5 38.7 %collective-permute-start.26 = (bf16[4,96,768]{2,1,0:T(8,128)(2,1)}, bf16[4,96,768]{2,1,0:T(8,128)(2,1)}, u32[]{:S(2)}, u32[]{:S(2)}) collective-permute-start(bf16[4,96,768]{2,1,0:T(8,128)(2,1)} %get-tuple-element.133), channel_id=1, source_target_pairs={{0,4},{4,0},{8,12},{12,8},{1,5},{5,1},{9,13},{13,9},{2,6},{6,2},{1... | collective-permute-start | bytes 1769480 | tf_op jit(solution)/shard_map/ppermute | solution.py:189
  241.0 68.7 %collective-permute-start.25 = (bf16[4,96,768]{2,1,0:T(8,128)(2,1)}, bf16[4,96,768]{2,1,0:T(8,128)(2,1)}, u32[]{:S(2)}, u32[]{:S(2)}) collective-permute-start(bf16[4,96,768]{2,1,0:T(8,128)(2,1)} %get-tuple-element.134), channel_id=1, source_target_pairs={{0,8},{4,12},{8,0},{12,4},{1,9},{5,13},{9,1},{13,5},{2,10},{6,14},... | collective-permute-start | bytes 1769480 | tf_op jit(solution)/shard_map/ppermute | solution.py:189
  242.6 14.6 %collective-permute-start.32 = (bf16[96,768]{1,0:T(8,128)(2,1)S(1)}, bf16[96,768]{1,0:T(8,128)(2,1)S(1)}, u32[]{:S(2)}, u32[]{:S(2)}) collective-permute-start(bf16[96,768]{1,0:T(8,128)(2,1)S(1)} %get-tuple-element.151), channel_id=1, source_target_pairs={{0,4},{4,0},{8,12},{12,8},{1,5},{5,1},{9,13},{13,9},{2,6},{6,2},{1... | collective-permute-start | bytes 442376 | tf_op jit(solution)/shard_map/ppermute | solution.py:189
  243.1 31.1 %collective-permute-start.31 = (bf16[96,768]{1,0:T(8,128)(2,1)S(1)}, bf16[96,768]{1,0:T(8,128)(2,1)S(1)}, u32[]{:S(2)}, u32[]{:S(2)}) collective-permute-start(bf16[96,768]{1,0:T(8,128)(2,1)S(1)} %get-tuple-element.152), channel_id=1, source_target_pairs={{0,8},{4,12},{8,0},{12,4},{1,9},{5,13},{9,1},{13,5},{2,10},{6,14},... | collective-permute-start | bytes 442376 | tf_op jit(solution)/shard_map/ppermute | solution.py:189
  244.6 31.1 %collective-permute-start.30 = (bf16[96,768]{1,0:T(8,128)(2,1)S(1)}, bf16[96,768]{1,0:T(8,128)(2,1)S(1)}, u32[]{:S(2)}, u32[]{:S(2)}) collective-permute-start(bf16[96,768]{1,0:T(8,128)(2,1)S(1)} %get-tuple-element.150), channel_id=1, source_target_pairs={{0,12},{4,8},{8,4},{12,0},{1,13},{5,9},{9,5},{13,1},{2,14},{6,10},... | collective-permute-start | bytes 442376 | tf_op jit(solution)/shard_map/ppermute | solution.py:189
  257.1 52.5 %collective-permute-start.24 = (bf16[4,96,768]{2,1,0:T(8,128)(2,1)}, bf16[4,96,768]{2,1,0:T(8,128)(2,1)}, u32[]{:S(2)}, u32[]{:S(2)}) collective-permute-start(bf16[4,96,768]{2,1,0:T(8,128)(2,1)} %get-tuple-element.132), channel_id=1, source_target_pairs={{0,12},{4,8},{8,4},{12,0},{1,13},{5,9},{9,5},{13,1},{2,14},{6,10},... | collective-permute-start | bytes 1769480 | tf_op jit(solution)/shard_map/ppermute | solution.py:189
  274.2 38.3 %collective-permute-start.29 = (bf16[4,96,768]{2,1,0:T(8,128)(2,1)}, bf16[4,96,768]{2,1,0:T(8,128)(2,1)}, u32[]{:S(2)}, u32[]{:S(2)}) collective-permute-start(bf16[4,96,768]{2,1,0:T(8,128)(2,1)} %get-tuple-element.130), channel_id=1, source_target_pairs={{0,4},{4,0},{8,12},{12,8},{1,5},{5,1},{9,13},{13,9},{2,6},{6,2},{1... | collective-permute-start | bytes 1769480 | tf_op jit(solution)/shard_map/ppermute | solution.py:189
  275.7 36.8 %collective-permute-start.28 = (bf16[4,96,768]{2,1,0:T(8,128)(2,1)}, bf16[4,96,768]{2,1,0:T(8,128)(2,1)}, u32[]{:S(2)}, u32[]{:S(2)}) collective-permute-start(bf16[4,96,768]{2,1,0:T(8,128)(2,1)} %get-tuple-element.131), channel_id=1, source_target_pairs={{0,8},{4,12},{8,0},{12,4},{1,9},{5,13},{9,1},{13,5},{2,10},{6,14},... | collective-permute-start | bytes 1769480 | tf_op jit(solution)/shard_map/ppermute | solution.py:189
  276.2 36.3 %collective-permute-start.27 = (bf16[4,96,768]{2,1,0:T(8,128)(2,1)}, bf16[4,96,768]{2,1,0:T(8,128)(2,1)}, u32[]{:S(2)}, u32[]{:S(2)}) collective-permute-start(bf16[4,96,768]{2,1,0:T(8,128)(2,1)} %get-tuple-element.129), channel_id=1, source_target_pairs={{0,12},{4,8},{8,4},{12,0},{1,13},{5,9},{9,5},{13,1},{2,14},{6,10},... | collective-permute-start | bytes 1769480 | tf_op jit(solution)/shard_map/ppermute | solution.py:189
  323.6 102.4 %reduce-scatter.2.cloned.1.call-start = ((), (), s32[]{:S(2)}) async-start(), calls=%async_computation.2 | async-start | bytes 1474560 | tf_op jit(solution)/shard_map/reduce_scatter | solution.py:395
  334.9 6.5 %collective-permute-start.41 = (bf16[384,576]{0,1:T(8,128)(2,1)}, bf16[384,576]{0,1:T(8,128)(2,1)}, u32[]{:S(2)}, u32[]{:S(2)}) collective-permute-start(bf16[384,576]{0,1:T(8,128)(2,1)} %bitcast.262), channel_id=1, source_target_pairs={{0,16},{16,0},{1,17},{17,1},{2,18},{18,2},{3,19},{19,3},{4,20},{20... | collective-permute-start | bytes 1327112 | tf_op jit(solution)/shard_map/ppermute | solution.py:189
  342.8 9.6 %collective-permute-start.44 = (bf16[96,576]{1,0:T(8,128)(2,1)S(1)}, bf16[96,576]{1,0:T(8,128)(2,1)S(1)}, u32[]{:S(2)}, u32[]{:S(2)}) collective-permute-start(bf16[96,576]{1,0:T(8,128)(2,1)S(1)} %get-tuple-element.154), channel_id=1, source_target_pairs={{0,1},{1,0},{2,3},{3,2},{4,5},{5,4},{6,7},{7,6},{8,9},{9,8},{10,11... | collective-permute-start | bytes 331784 | tf_op jit(solution)/shard_map/ppermute | solution.py:189
  345.2 14.5 %collective-permute-start.43 = (bf16[96,576]{1,0:T(8,128)(2,1)S(1)}, bf16[96,576]{1,0:T(8,128)(2,1)S(1)}, u32[]{:S(2)}, u32[]{:S(2)}) collective-permute-start(bf16[96,576]{1,0:T(8,128)(2,1)S(1)} %get-tuple-element.155), channel_id=1, source_target_pairs={{0,2},{1,3},{2,0},{3,1},{4,6},{5,7},{6,4},{7,5},{8,10},{9,11},{10,... | collective-permute-start | bytes 331784 | tf_op jit(solution)/shard_map/ppermute | solution.py:189
  347.7 12.0 %collective-permute-start.42 = (bf16[96,576]{1,0:T(8,128)(2,1)S(1)}, bf16[96,576]{1,0:T(8,128)(2,1)S(1)}, u32[]{:S(2)}, u32[]{:S(2)}) collective-permute-start(bf16[96,576]{1,0:T(8,128)(2,1)S(1)} %get-tuple-element.153), channel_id=1, source_target_pairs={{0,3},{1,2},{2,1},{3,0},{4,7},{5,6},{6,5},{7,4},{8,11},{9,10},{10,... | collective-permute-start | bytes 331784 | tf_op jit(solution)/shard_map/ppermute | solution.py:189
  347.7 22.3 %copy-start.49 = (f32[512,1536]{1,0:T(8,128)S(1)}, f32[512,1536]{1,0:T(8,128)}, u32[]{:S(2)}) copy-start(f32[512,1536]{1,0:T(8,128)} %copy-done.48) | copy-start | bytes 9437188
  347.7 22.3 %copy-start.50 = (f32[512,768]{1,0:T(8,128)S(1)}, f32[512,768]{1,0:T(8,128)}, u32[]{:S(2)}) copy-start(f32[512,768]{1,0:T(8,128)} %fusion.50) | copy-start | bytes 4718596
  352.4 11.6 %copy-start.16 = (bf16[2048,768]{1,0:T(8,128)(2,1)}, bf16[2048,768]{1,0:T(8,128)(2,1)S(1)}, u32[]{:S(2)}) copy-start(bf16[2048,768]{1,0:T(8,128)(2,1)S(1)} %convolution_convert_fusion.2) | copy-start | bytes 9437188
  359.7 8.2 %collective-permute-start.45 = (bf16[96,576]{1,0:T(8,128)(2,1)S(1)}, bf16[96,576]{1,0:T(8,128)(2,1)S(1)}, u32[]{:S(2)}, u32[]{:S(2)}) collective-permute-start(bf16[96,576]{1,0:T(8,128)(2,1)S(1)} %fusion.44), channel_id=1, source_target_pairs={{0,1},{1,0},{2,3},{3,2},{4,5},{5,4},{6,7},{7,6},{8,9},{9,8},{10,11... | collective-permute-start | bytes 331784 | tf_op jit(solution)/shard_map/ppermute | solution.py:189
  364.0 45.4 %collective-permute-start.35 = (bf16[512,768]{1,0:T(8,128)(2,1)}, bf16[512,768]{1,0:T(8,128)(2,1)S(1)}, u32[]{:S(2)}, u32[]{:S(2)}) collective-permute-start(bf16[512,768]{1,0:T(8,128)(2,1)} %get-tuple-element.127), channel_id=1, source_target_pairs={{0,4},{4,0},{8,12},{12,8},{1,5},{5,1},{9,13},{13,9},{2,6},{6,2},{1... | collective-permute-start | bytes 2359304 | tf_op jit(solution)/shard_map/ppermute | solution.py:189
  365.5 45.8 %collective-permute-start.34 = (bf16[512,768]{1,0:T(8,128)(2,1)}, bf16[512,768]{1,0:T(8,128)(2,1)}, u32[]{:S(2)}, u32[]{:S(2)}) collective-permute-start(bf16[512,768]{1,0:T(8,128)(2,1)} %get-tuple-element.128), channel_id=1, source_target_pairs={{0,8},{4,12},{8,0},{12,4},{1,9},{5,13},{9,1},{13,5},{2,10},{6,14},... | collective-permute-start | bytes 2359304 | tf_op jit(solution)/shard_map/ppermute | solution.py:189
  366.0 45.3 %collective-permute-start.33 = (bf16[512,768]{1,0:T(8,128)(2,1)}, bf16[512,768]{1,0:T(8,128)(2,1)}, u32[]{:S(2)}, u32[]{:S(2)}) collective-permute-start(bf16[512,768]{1,0:T(8,128)(2,1)} %get-tuple-element.126), channel_id=1, source_target_pairs={{0,12},{4,8},{8,4},{12,0},{1,13},{5,9},{9,5},{13,1},{2,14},{6,10},... | collective-permute-start | bytes 2359304 | tf_op jit(solution)/shard_map/ppermute | solution.py:189
  367.6 16.3 %collective-permute-start.46 = (bf16[96,576]{1,0:T(8,128)(2,1)S(1)}, bf16[96,576]{1,0:T(8,128)(2,1)S(1)}, u32[]{:S(2)}, u32[]{:S(2)}) collective-permute-start(bf16[96,576]{1,0:T(8,128)(2,1)S(1)} %fusion.44), channel_id=1, source_target_pairs={{0,2},{1,3},{2,0},{3,1},{4,6},{5,7},{6,4},{7,5},{8,10},{9,11},{10,... | collective-permute-start | bytes 331784 | tf_op jit(solution)/shard_map/ppermute | solution.py:189
  368.0 16.1 %collective-permute-start.47 = (bf16[96,576]{1,0:T(8,128)(2,1)S(1)}, bf16[96,576]{1,0:T(8,128)(2,1)S(1)}, u32[]{:S(2)}, u32[]{:S(2)}) collective-permute-start(bf16[96,576]{1,0:T(8,128)(2,1)S(1)} %fusion.44), channel_id=1, source_target_pairs={{0,3},{1,2},{2,1},{3,0},{4,7},{5,6},{6,5},{7,4},{8,11},{9,10},{10,... | collective-permute-start | bytes 331784 | tf_op jit(solution)/shard_map/ppermute | solution.py:189
  405.6 13.3 %collective-permute-start.48 = (bf16[384,3,192]{0,2,1:T(8,128)(2,1)}, bf16[384,3,192]{0,2,1:T(8,128)(2,1)S(1)}, u32[]{:S(2)}, u32[]{:S(2)}) collective-permute-start(bf16[384,3,192]{0,2,1:T(8,128)(2,1)} %reshape_reshape.3), channel_id=1, source_target_pairs={{0,4},{4,0},{8,12},{12,8},{1,5},{5,1},{9,13},{13,9},{2,6},{6,2},{1... | collective-permute-start | bytes 1327112 | tf_op jit(solution)/shard_map/ppermute | solution.py:189
  407.1 18.0 %collective-permute-start.49 = (bf16[384,3,192]{0,2,1:T(8,128)(2,1)}, bf16[384,3,192]{0,2,1:T(8,128)(2,1)S(1)}, u32[]{:S(2)}, u32[]{:S(2)}) collective-permute-start(bf16[384,3,192]{0,2,1:T(8,128)(2,1)} %reshape_reshape.3), channel_id=1, source_target_pairs={{0,8},{4,12},{8,0},{12,4},{1,9},{5,13},{9,1},{13,5},{2,10},{6,14},... | collective-permute-start | bytes 1327112 | tf_op jit(solution)/shard_map/ppermute | solution.py:189
  409.4 20.0 %collective-permute-start.50 = (bf16[384,3,192]{0,2,1:T(8,128)(2,1)}, bf16[384,3,192]{0,2,1:T(8,128)(2,1)}, u32[]{:S(2)}, u32[]{:S(2)}) collective-permute-start(bf16[384,3,192]{0,2,1:T(8,128)(2,1)} %reshape_reshape.3), channel_id=1, source_target_pairs={{0,12},{4,8},{8,4},{12,0},{1,13},{5,9},{9,5},{13,1},{2,14},{6,10},... | collective-permute-start | bytes 1327112 | tf_op jit(solution)/shard_map/ppermute | solution.py:189
  429.3 1.9 collective-permute-start.36
  431.3 4.2 collective-permute-start.37
  435.5 4.2 collective-permute-start.38
  436.5 28.8 %collective-permute-start.51 = (bf16[288,768]{1,0:T(8,128)(2,1)}, bf16[288,768]{1,0:T(8,128)(2,1)}, u32[]{:S(2)}, u32[]{:S(2)}) collective-permute-start(bf16[288,768]{1,0:T(8,128)(2,1)} %constant_dynamic-update-slice_fusion.3), channel_id=1, source_target_pairs={{0,4},{4,0},{8,12},{12,8},{1,5},{5,1},{9,13},{13,9},{2,6},{6,2},{1... | collective-permute-start | bytes 1327112 | tf_op jit(solution)/shard_map/ppermute | solution.py:189
  440.2 16.7 %collective-permute-start.39 = (f32[12,768]{1,0:T(8,128)}, f32[12,768]{1,0:T(8,128)}, u32[]{:S(2)}, u32[]{:S(2)}) collective-permute-start(f32[12,768]{1,0:T(8,128)} %add.399), channel_id=1, source_target_pairs={{0,1},{1,0},{2,3},{3,2},{4,5},{5,4},{6,7},{7,6},{8,9},{9,8},{10,11... | collective-permute-start | bytes 110600 | tf_op jit(solution)/shard_map/ppermute | solution.py:189
  455.0 20.0 %collective-permute-start.52 = (bf16[288,768]{1,0:T(8,128)(2,1)}, bf16[288,768]{1,0:T(8,128)(2,1)S(1)}, u32[]{:S(2)}, u32[]{:S(2)}) collective-permute-start(bf16[288,768]{1,0:T(8,128)(2,1)} %constant_dynamic-update-slice_fusion.3), channel_id=1, source_target_pairs={{0,8},{4,12},{8,0},{12,4},{1,9},{5,13},{9,1},{13,5},{2,10},{6,14},... | collective-permute-start | bytes 1327112 | tf_op jit(solution)/shard_map/ppermute | solution.py:189
  455.0 20.1 %collective-permute-start.53 = (bf16[288,768]{1,0:T(8,128)(2,1)}, bf16[288,768]{1,0:T(8,128)(2,1)S(1)}, u32[]{:S(2)}, u32[]{:S(2)}) collective-permute-start(bf16[288,768]{1,0:T(8,128)(2,1)} %constant_dynamic-update-slice_fusion.3), channel_id=1, source_target_pairs={{0,12},{4,8},{8,4},{12,0},{1,13},{5,9},{9,5},{13,1},{2,14},{6,10},... | collective-permute-start | bytes 1327112 | tf_op jit(solution)/shard_map/ppermute | solution.py:189
  457.8 5.4 %collective-permute-start.40 = (f32[12,768]{1,0:T(8,128)S(1)}, f32[12,768]{1,0:T(8,128)S(1)}, u32[]{:S(2)}, u32[]{:S(2)}) collective-permute-start(f32[12,768]{1,0:T(8,128)S(1)} %add.400), channel_id=1, source_target_pairs={{0,2},{1,3},{2,0},{3,1},{4,6},{5,7},{6,4},{7,5},{8,10},{9,11},{10,... | collective-permute-start | bytes 110600 | tf_op jit(solution)/shard_map/ppermute | solution.py:189
  (44 other events, 191.6 us)
Sparse Core Ops, SparseCore 0:
  32.2 50.4 all-gather.2
  323.7 37.3 all-reduce.1
  364.1 33.8 reduce-scatter.1
